TPU v7x, 32 devices: a whole 2x2x4 slice. The times are simulated.
32 devices in a mesh: ang: 16 (over z, y, core), sl: 2 (over x).
Axes of the slice: x: 2, y: 2, z: 4, core: 2. Of those that a mesh axis runs over, the one named last changes fastest.
Arguments:
- projections: float32 [32, 8, 4352], P('ang', 'sl'), may hold values from -6 to 6
- partner: int32 [32], replicated, may hold values from 0 to 31, as said below
- offsets: int32 [32], P('ang'), may hold values from 0 to 192
- angles: float32 [32], replicated, may hold values from 0 to 6.2832, as said below
- coefficients: float32 [2, 8, 4096, 1280], P(None, None, ('ang', 'sl')), may hold values from -6 to 6
Outputs:
- updated: float32 [2, 8, 4096, 1280], P(None, None, ('ang', 'sl'))
- misfit: float32 [32, 8], P('ang', 'sl')
Inputs may be any that keep to these rules, and one draw needn't show every extreme that they name: partner[partner[g]] = g, and g // 2 and partner[g] // 2 differ by 8: a projection's partner lies on the index of ang half the axis away. angles[partner[g]] lies within pi / 16 of angles[g] + pi or angles[g] - pi.
All inputs are finite; a program needn't handle non-finite values.
Results may differ from a plain program's by a relative error of at most 0.0003.
Values sent between devices are 32-bit elements; how exact they have to be, the bound alone decides.
A program may use at most 64 MiB of HBM per device.

v0:
```python
import functools
import math

import jax
import jax.numpy as jnp
import ml_dtypes
import numpy as np
from jax import lax
from jax.experimental import pallas as pl
from jax.experimental.pallas import tpu as pltpu
from jax.sharding import PartitionSpec as P

W = 8192
HALF = 4096
K = 4096
EXTRA = 256
RAMP = 64
ROWS = 8


paganin_strength = 16.0
small_eps = 1e-06
highest = lax.Precision.HIGHEST


def from_behind(value, axis, steps):
    count = lax.axis_size(axis)
    pairs = [(source, (source + steps) % count) for source in range(count)]
    return lax.ppermute(value, axis, pairs)


def paganin_rows(frequencies):
    row_ids = jnp.arange(ROWS, dtype=jnp.int32)
    row_offset = (row_ids[:, None] - row_ids[None, :]) % ROWS
    cos_table = jnp.cos(
        2.0
        * math.pi
        / ROWS
        * (row_ids[:, None, None] * row_offset[None, :, :] % ROWS).astype(jnp.float32)
    )
    row_freq = jnp.minimum(row_ids, ROWS - row_ids).astype(jnp.float32) / ROWS
    col_freq = frequencies / W
    damping = 1.0 / (
        1.0
        + paganin_strength
        * (col_freq[:, None] * col_freq[:, None] + row_freq[None, :] * row_freq[None, :])
    )
    return jnp.einsum("nq,qij->nij", damping, cos_table, precision=highest) / ROWS


def blend_band(projections, mirrored, offsets):
    position = jnp.arange(EXTRA, dtype=jnp.int32).astype(jnp.float32)
    weight = jnp.clip((position[None, :] - offsets[:, None].astype(jnp.float32)) / RAMP, 0.0, 1.0)
    own_band = projections[:, :, HALF - EXTRA : HALF]
    blended = own_band + weight[:, None, :] * (mirrored - own_band)
    return jnp.concatenate([projections[:, :, : HALF - EXTRA], blended], axis=2)


def spectrum_of(stitched):
    row_count = stitched.shape[0] * stitched.shape[1]
    low_split = W // 128
    outer_count = HALF // low_split
    high_count = K // 128
    folded = stitched.reshape(row_count, outer_count, low_split)
    norm_scale = 1.0 / math.sqrt(HALF)
    outer_ids = jnp.arange(outer_count, dtype=jnp.int32)
    lane_ids = jnp.arange(128, dtype=jnp.int32)
    first_phase = (
        2.0 * math.pi / 128 * (outer_ids[:, None] * lane_ids[None, :] % 128).astype(jnp.float32)
    )
    first_cos = jnp.cos(first_phase) * norm_scale
    first_sin = jnp.sin(first_phase) * norm_scale
    part_real = jnp.einsum("rab,ap->rbp", folded, first_cos, precision=highest)
    part_imag = -jnp.einsum("rab,ap->rbp", folded, first_sin, precision=highest)
    low_ids = jnp.arange(low_split, dtype=jnp.int32)
    twist_phase = 2.0 * math.pi / W * (low_ids[:, None] * lane_ids[None, :]).astype(jnp.float32)
    twist_cos = jnp.cos(twist_phase)
    twist_sin = jnp.sin(twist_phase)
    turned_real = part_real * twist_cos + part_imag * twist_sin
    turned_imag = part_imag * twist_cos - part_real * twist_sin
    high_ids = jnp.arange(high_count, dtype=jnp.int32)
    last_phase = (
        2.0
        * math.pi
        / low_split
        * (low_ids[:, None] * high_ids[None, :] % low_split).astype(jnp.float32)
    )
    last_cos = jnp.cos(last_phase)
    last_sin = jnp.sin(last_phase)
    spec_real = jnp.einsum("rbp,bq->rqp", turned_real, last_cos, precision=highest) + jnp.einsum(
        "rbp,bq->rqp", turned_imag, last_sin, precision=highest
    )
    spec_imag = jnp.einsum("rbp,bq->rqp", turned_imag, last_cos, precision=highest) - jnp.einsum(
        "rbp,bq->rqp", turned_real, last_sin, precision=highest
    )
    out_shape = (stitched.shape[0], stitched.shape[1], K)
    return (spec_real.reshape(out_shape), spec_imag.reshape(out_shape))


def apply_rows(harm_table, coef_part):
    return jnp.einsum("gm,cm->gc", harm_table, coef_part, precision=highest)


def apply_back(harm_table, resid_part):
    return jnp.einsum("gm,gc->cm", harm_table, resid_part, precision=highest)


def shards(projections, partner, offsets, angles, coefficients):
    ang_count = lax.axis_size("ang")
    sl_count = lax.axis_size("sl")
    ang_index = lax.axis_index("ang")
    sl_index = lax.axis_index("sl")
    per_dev = projections.shape[0]
    rows_dev = projections.shape[1]
    total_angles = per_dev * ang_count
    block_freqs = coefficients.shape[2]
    harmonics = coefficients.shape[3]
    columns = ROWS * block_freqs
    own_partners = lax.dynamic_slice_in_dim(partner, ang_index * per_dev, per_dev)
    across_dev = (ang_index + ang_count // 2) % ang_count
    partner_slots = own_partners - across_dev * per_dev
    arrived = from_behind(projections[:, :, HALF:], "ang", ang_count // 2)
    mirrored = jnp.flip(jnp.take(arrived, partner_slots, axis=0), axis=2)
    stitched = blend_band(projections, mirrored, offsets)
    spec_real, spec_imag = spectrum_of(stitched)
    spectra = jnp.stack([spec_real, spec_imag])
    layered = spectra.reshape(2, per_dev, rows_dev, ang_count, sl_count, block_freqs)
    by_rows = lax.all_to_all(layered, "sl", split_axis=4, concat_axis=2, tiled=True)
    regrouped = lax.all_to_all(by_rows, "ang", split_axis=3, concat_axis=1, tiled=True)
    freq_major = regrouped.reshape(2, total_angles, columns)
    freq_base = (ang_index * sl_count + sl_index) * block_freqs
    local_freq = (freq_base + jnp.arange(block_freqs, dtype=jnp.int32)).astype(jnp.float32)
    col_freq = jnp.tile(local_freq, ROWS)
    turn_phase = 2.0 * math.pi / W * col_freq
    turn_cos = jnp.cos(turn_phase)
    turn_sin = jnp.sin(turn_phase)
    own_real = freq_major[0]
    own_imag = freq_major[1]
    pair_real = jnp.take(own_real, partner, axis=0)
    pair_imag = jnp.take(own_imag, partner, axis=0)
    comb_real = own_real + turn_cos * pair_real + turn_sin * pair_imag
    comb_imag = own_imag + turn_sin * pair_real - turn_cos * pair_imag
    rows_matrix = paganin_rows(local_freq)
    full_matrix = jnp.einsum(
        "nij,mn->jmin", rows_matrix, jnp.eye(block_freqs, dtype=jnp.float32)
    ).reshape(columns, columns)
    filt_real = jnp.dot(comb_real, full_matrix, precision=highest)
    filt_imag = jnp.dot(comb_imag, full_matrix, precision=highest)
    ramp_weights = (col_freq + 0.5) / K
    coef_real = coefficients[0].reshape(columns, harmonics)
    coef_imag = coefficients[1].reshape(columns, harmonics)
    block_count = total_angles // total_angles
    harm_shift = (jnp.arange(harmonics, dtype=jnp.int32) - harmonics // 2).astype(jnp.float32)
    norm_scale = 1.0 / math.sqrt(harmonics)

    def harmonic_tables():
        phase_tab = angles[:, None] * harm_shift[None, :]
        return (jnp.cos(phase_tab) * norm_scale, jnp.sin(phase_tab) * norm_scale)

    def first_pass(running, block_index):
        grad_real, grad_imag = running
        cos_tab, sin_tab = harmonic_tables()
        model_real = apply_rows(cos_tab, coef_real) - apply_rows(sin_tab, coef_imag)
        model_imag = apply_rows(cos_tab, coef_imag) + apply_rows(sin_tab, coef_real)
        diff_real = model_real - filt_real
        diff_imag = model_imag - filt_imag
        resid_real = ramp_weights * diff_real
        resid_imag = ramp_weights * diff_imag
        energy = (diff_real * resid_real + diff_imag * resid_imag).reshape(
            total_angles, ROWS, block_freqs
        )
        partial_rows = jnp.sum(energy, axis=2) / K
        grad_real = grad_real + apply_back(cos_tab, resid_real) + apply_back(sin_tab, resid_imag)
        grad_imag = grad_imag + apply_back(cos_tab, resid_imag) - apply_back(sin_tab, resid_real)
        return ((grad_real, grad_imag), partial_rows)

    zero_grad = jnp.zeros((columns, harmonics), jnp.float32)
    block_ids = jnp.arange(block_count, dtype=jnp.int32)
    grads, partial_table = lax.scan(first_pass, (zero_grad, zero_grad), block_ids)
    grad_real, grad_imag = grads
    misfit_table = partial_table.reshape(total_angles, ROWS)

    def second_pass(running_sum, block_index):
        cos_tab, sin_tab = harmonic_tables()
        image_real = apply_rows(cos_tab, grad_real) - apply_rows(sin_tab, grad_imag)
        image_imag = apply_rows(cos_tab, grad_imag) + apply_rows(sin_tab, grad_real)
        return (
            running_sum
            + jnp.sum(ramp_weights * (image_real * image_real + image_imag * image_imag)),
            block_index,
        )

    curvature, unused = lax.scan(second_pass, jnp.float32(0.0), block_ids)
    grad_norm = jnp.sum(grad_real * grad_real + grad_imag * grad_imag)
    arranged = (
        misfit_table.reshape(ang_count, per_dev, sl_count, rows_dev)
        .transpose(0, 2, 1, 3)
        .reshape(ang_count * sl_count, per_dev, rows_dev)
    )
    misfit = lax.psum_scatter(arranged, ("ang", "sl"), scatter_dimension=0, tiled=True)[0]
    grad_total, curv_total = lax.psum((grad_norm, curvature), ("ang", "sl"))
    step_size = grad_total / (curv_total + small_eps)
    step_grad = jnp.stack([grad_real, grad_imag]).reshape(2, ROWS, block_freqs, harmonics)
    updated = coefficients - step_size * step_grad
    return (updated, misfit)


LANES = 128
MESH = pl.DeviceIdType.MESH
NT = (((1,), (1,)), ((), ()))
f32 = jnp.float32
bf16 = jnp.bfloat16


def halves(value):
    high = value.astype(bf16)
    return high, (value - high.astype(f32)).astype(bf16)


def np_halves(value):
    value = value.astype(np.float32)
    high = value.astype(ml_dtypes.bfloat16)
    return high, (value - high.astype(np.float32)).astype(ml_dtypes.bfloat16)


def transform_tables():
    outer = HALF // LANES
    ids = np.arange(64)[:, None] * np.arange(outer)[None, :] % 64
    phase = 2.0 * np.pi / 64 * ids
    first = np.concatenate([np.cos(phase), -np.sin(phase)]) / math.sqrt(HALF)
    high, low = np_halves(first)
    first = np.concatenate([high, high, low, low], axis=1)
    lane = np.arange(LANES)
    phase = 2.0 * np.pi / W * (lane[:, None] * lane[None, :])
    twist = np.stack([np.cos(phase), np.sin(phase)]).astype(np.float32)
    phase = 2.0 * np.pi / 64 * (np.arange(K // LANES)[:, None] * lane[None, :] % 64)
    last = np.concatenate(
        [
            np.concatenate([np.cos(phase), np.sin(phase)], axis=1),
            np.concatenate([-np.sin(phase), np.cos(phase)], axis=1),
        ]
    )
    return first, twist, np.concatenate(np_halves(last))


def cos_sin(phase):
    turns = jnp.floor(phase * (2.0 / math.pi) + 0.5)
    rest = phase - turns * 1.5703125
    rest = rest - turns * 4.837512969970703125e-4
    rest = rest - turns * 7.54978995489188216e-8
    square = rest * rest
    sine = rest + rest * square * (
        -1.6666654611e-1 + square * (8.3321608736e-3 + square * -1.9515295891e-4)
    )
    cosine = (
        1.0
        - 0.5 * square
        + square
        * square
        * (4.166664568298827e-2 + square * (-1.388731625493765e-3 + square * 2.443315711809948e-5))
    )
    quarter = turns - 4.0 * jnp.floor(turns * 0.25)
    odd = (quarter == 1.0) | (quarter == 3.0)
    base_cos = jnp.where(odd, sine, cosine)
    base_sin = jnp.where(odd, cosine, sine)
    cos_out = jnp.where((quarter == 1.0) | (quarter == 2.0), -base_cos, base_cos)
    sin_out = jnp.where(quarter >= 2.0, -base_sin, base_sin)
    return cos_out, sin_out


def residual_kernel(
    ang_count,
    sl_count,
    partner,
    offsets,
    angles,
    proj,
    first_tab,
    twist_tab,
    last_tab,
    coef,
    left_out,
    harm_out,
    table_out,
    coef_buf,
    model_buf,
    band,
    folded,
    send_buf,
    recv_buf,
    share_buf,
    harm_rows,
    coef_sem,
    band_send,
    band_recv,
    spec_send,
    spec_recv,
    share_send,
    share_recv,
):
    count = ang_count * sl_count
    per_dev, rows_dev = proj.shape[0], proj.shape[1]
    total = per_dev * ang_count
    own_rows = per_dev * rows_dev
    harmonics = coef.shape[2]
    columns = coef.shape[1]
    chunk = columns // 4
    ang = lax.axis_index("ang")
    sl = lax.axis_index("sl")
    me = ang * sl_count + sl

    def coef_copy(part, index):
        rows = pl.ds(index * chunk, chunk)
        return pltpu.make_async_copy(
            coef.at[part, rows], coef_buf.at[part, rows], coef_sem.at[part, index]
        )

    for index in range(4):
        for part in range(2):
            coef_copy(part, index).start()

    barrier = pltpu.get_barrier_semaphore()

    def greet(step, carry):
        other = lax.rem(me + step, count)
        pl.semaphore_signal(
            barrier,
            inc=1,
            device_id=(other // sl_count, lax.rem(other, sl_count)),
            device_id_type=MESH,
        )
        return carry

    lax.fori_loop(1, count, greet, 0)

    row_id = lax.broadcasted_iota(jnp.int32, (total, LANES), 0)
    angle_rows = jnp.zeros((total, LANES), f32)
    slot_rows = jnp.zeros((total, LANES), f32)
    for g in range(total):
        place = (g % per_dev) * ang_count + g // per_dev
        hit = row_id == place
        angle_rows = jnp.where(hit, angles[g], angle_rows)
        slot_rows = jnp.where(hit, (partner[g] % per_dev).astype(f32), slot_rows)

    pl.semaphore_wait(barrier, count - 1)
    across = lax.rem(ang + ang_count // 2, ang_count)
    band_copy = pltpu.make_async_remote_copy(
        src_ref=proj.at[:, :, pl.ds(HALF, EXTRA)],
        dst_ref=band,
        send_sem=band_send,
        recv_sem=band_recv,
        device_id=(across, sl),
        device_id_type=MESH,
    )
    band_copy.start()

    lane_id = lax.broadcasted_iota(jnp.int32, (total, LANES), 1)
    scale = 1.0 / math.sqrt(harmonics)
    for tile in range(harmonics // LANES):
        at = pl.ds(tile * LANES, LANES)
        shift = (lane_id + (tile * LANES - harmonics // 2)).astype(f32)
        cos_tab, sin_tab = cos_sin(angle_rows * shift)
        cos_tab = cos_tab * scale
        sin_tab = sin_tab * scale
        for part, stacked in enumerate(
            (
                jnp.concatenate([cos_tab, sin_tab], axis=0),
                jnp.concatenate([-sin_tab, cos_tab], axis=0),
            )
        ):
            high, low = halves(stacked)
            harm_rows[part, :, at] = jnp.concatenate([high, low], axis=0)
            harm_out[part, :, at] = jnp.concatenate([high, high, low, low], axis=0)

    flat_lanes = (HALF - EXTRA) // LANES
    outer = HALF // LANES
    for g in range(per_dev):
        for tile in range(flat_lanes):
            folded[pl.ds(g * rows_dev * outer + tile, rows_dev, stride=outer), :] = proj[
                g, :, pl.ds(tile * LANES, LANES)
            ]
    gram = lax.dot_general(harm_rows[0], harm_rows[0], NT, preferred_element_type=f32)
    gram = gram + lax.dot_general(harm_rows[1], harm_rows[1], NT, preferred_element_type=f32)
    width = 2 * total
    gram = gram[:width] + gram[width:]
    gram = gram + pltpu.roll(gram, width, 1)
    gram_high, gram_low = halves(gram)
    gram_rows = jnp.concatenate([gram_high, gram_high, gram_low, gram_low], axis=0)

    band_copy.wait_recv()
    flip = (
        lax.broadcasted_iota(jnp.int32, (EXTRA, EXTRA), 0)
        + lax.broadcasted_iota(jnp.int32, (EXTRA, EXTRA), 1)
        == EXTRA - 1
    ).astype(f32)
    mirrored = jnp.dot(
        jnp.concatenate([band[g] for g in range(per_dev)], axis=0),
        flip,
        precision=highest,
        preferred_element_type=f32,
    )
    position = lax.broadcasted_iota(jnp.int32, (rows_dev, EXTRA), 1).astype(f32)
    for g in range(per_dev):
        slot = partner[ang * per_dev + g] % per_dev
        slot = jnp.full((rows_dev, EXTRA), slot.astype(f32))
        pick = mirrored[:rows_dev]
        for other in range(1, per_dev):
            pick = jnp.where(
                slot == float(other), mirrored[other * rows_dev : (other + 1) * rows_dev], pick
            )
        own = proj[g, :, pl.ds(HALF - EXTRA, EXTRA)]
        weight = jnp.clip((position - offsets[g].astype(f32)) / RAMP, 0.0, 1.0)
        mixed = own + weight * (pick - own)
        for tile in range(EXTRA // LANES):
            folded[pl.ds(g * rows_dev * outer + flat_lanes + tile, rows_dev, stride=outer), :] = (
                mixed[:, tile * LANES : (tile + 1) * LANES]
            )

    row_parts = []
    for row in range(own_rows):
        high, low = halves(folded[pl.ds(row * outer, outer), :])
        row_parts.append(jnp.concatenate([high, low, high, low], axis=0))
    first = jnp.dot(
        first_tab[...], jnp.concatenate(row_parts, axis=1), preferred_element_type=f32
    )
    twist_cos, twist_sin = twist_tab[0], twist_tab[1]
    last = last_tab[...]
    freqs = K // LANES
    for row in range(own_rows):
        real = first[:64, row * LANES : (row + 1) * LANES]
        imag = first[64:, row * LANES : (row + 1) * LANES]
        real = jnp.concatenate([real, real], axis=0)
        imag = jnp.concatenate([imag, imag], axis=0)
        turned = jnp.concatenate(
            [real * twist_cos + imag * twist_sin, imag * twist_cos - real * twist_sin], axis=1
        )
        high, low = halves(turned)
        by_high = lax.dot_general(last, high, NT, preferred_element_type=f32)
        by_low = lax.dot_general(last[: 2 * freqs], low, NT, preferred_element_type=f32)
        spec = by_high[: 2 * freqs] + by_high[2 * freqs :] + by_low
        for part in range(2):
            send_buf[pl.ds(part * own_rows + row, freqs, stride=2 * own_rows), :] = spec[
                part * freqs : (part + 1) * freqs
            ]

    block = 2 * own_rows

    def spec_copy(step):
        other = lax.rem(me + step, count)
        return pltpu.make_async_remote_copy(
            src_ref=send_buf.at[pl.ds(pl.multiple_of(other * block, block), block)],
            dst_ref=recv_buf.at[pl.ds(pl.multiple_of(me * block, block), block)],
            send_sem=spec_send.at[step],
            recv_sem=spec_recv.at[step],
            device_id=(other // sl_count, lax.rem(other, sl_count)),
            device_id_type=MESH,
        )

    def spec_arrival(step):
        source = lax.rem(me - step + count, count)
        return pltpu.make_async_remote_copy(
            src_ref=send_buf.at[pl.ds(pl.multiple_of(source * block, block), block)],
            dst_ref=recv_buf.at[pl.ds(pl.multiple_of(source * block, block), block)],
            send_sem=spec_send.at[step],
            recv_sem=spec_recv.at[step],
            device_id=(source // sl_count, lax.rem(source, sl_count)),
            device_id_type=MESH,
        )

    def start_spec(step, carry):
        spec_copy(step).start()
        return carry

    lax.fori_loop(1, count, start_spec, 0)
    mine = pl.ds(pl.multiple_of(me * block, block), block)
    recv_buf[mine, :] = send_buf[mine, :]

    def model_chunk(index, carry):
        found = None
        for part in range(2):
            coef_copy(part, index).wait()
            value = coef_buf[part, pl.ds(pl.multiple_of(index * chunk, chunk), chunk), :]
            high, low = halves(value)
            both = jnp.concatenate([high, low], axis=0)
            term = lax.dot_general(both, harm_rows[part], NT, preferred_element_type=f32)
            term = term[:chunk] + term[chunk:]
            found = term if found is None else found + term
        found = found + pltpu.roll(found, width, 1)
        model_buf[pl.ds(pl.multiple_of(index * chunk, chunk), chunk), :] = found
        return carry

    lax.fori_loop(0, 4, model_chunk, 0)

    base = (me * LANES).astype(f32)
    lane_freq = lax.broadcasted_iota(jnp.int32, (8, LANES), 1).astype(f32) + base
    turn_cos, turn_sin = cos_sin(2.0 * math.pi / W * lane_freq)
    turn_cos, turn_sin = turn_cos[:1], turn_sin[:1]
    col_freq = lane_freq[:1] / W
    damping = [
        1.0 / (1.0 + paganin_strength * (col_freq * col_freq + (q / ROWS) * (q / ROWS)))
        for q in range(5)
    ]
    mix = []
    for apart in range(5):
        entry = damping[0] + (1.0 if apart % 2 == 0 else -1.0) * damping[4]
        for q in range(1, 4):
            entry = entry + 2.0 * math.cos(2.0 * math.pi * q * apart / ROWS) * damping[q]
        mix.append(entry / ROWS)

    def wait_spec(step, carry):
        spec_arrival(step).wait_recv()
        return carry

    lax.fori_loop(1, count, wait_spec, 0)

    def rows_of(part, g, i):
        s, low_i = i // rows_dev, i % rows_dev
        start = s * block + part * own_rows + g * rows_dev + low_i
        return recv_buf[pl.ds(start, ang_count, stride=sl_count * block), :]

    def swapped(value):
        return jnp.concatenate([value[ang_count // 2 :], value[: ang_count // 2]], axis=0)

    comb = []
    for i in range(ROWS):
        own = [jnp.concatenate([rows_of(part, g, i) for g in range(per_dev)]) for part in range(2)]
        pair = []
        for part in range(2):
            behind = [
                swapped(own[part][g * ang_count : (g + 1) * ang_count]) for g in range(per_dev)
            ]
            pick = jnp.concatenate([behind[0]] * per_dev, axis=0)
            for g in range(1, per_dev):
                pick = jnp.where(
                    slot_rows == float(g), jnp.concatenate([behind[g]] * per_dev, axis=0), pick
                )
            pair.append(pick)
        comb.append(
            jnp.concatenate(
                [
                    own[0] + turn_cos * pair[0] + turn_sin * pair[1],
                    own[1] + turn_sin * pair[0] - turn_cos * pair[1],
                ],
                axis=0,
            )
        )

    weight = (
        lax.broadcasted_iota(jnp.int32, (LANES, LANES), 0).astype(f32) + (base + 0.5)
    ) / K
    share_row = lax.broadcasted_iota(jnp.int32, (ROWS, LANES), 0)
    share_lane = lax.broadcasted_iota(jnp.int32, (ROWS, LANES), 1)
    share = jnp.zeros((ROWS, LANES), f32)
    norm_rows = jnp.zeros((1, LANES), f32)
    curv_rows = jnp.zeros((1, LANES), f32)
    front = lax.broadcasted_iota(jnp.int32, (LANES, LANES), 1) < width
    for i in range(ROWS):
        filt = mix[0] * comb[i] + mix[4] * comb[(i + 4) % ROWS]
        for apart in range(1, 4):
            filt = filt + mix[apart] * (comb[(i + apart) % ROWS] + comb[(i - apart) % ROWS])
        filt = jnp.transpose(jnp.concatenate([filt, filt], axis=0))
        diff = model_buf[i * LANES : (i + 1) * LANES, :] - filt
        resid = weight * diff
        energy = jnp.sum(diff * resid, axis=0, keepdims=True) / K
        energy = energy + pltpu.roll(energy, LANES - total, 1)
        share = jnp.where((share_row == i) & (share_lane < total), energy, share)
        high = resid.astype(bf16).astype(f32)
        packed = jnp.where(front, high, resid - high).astype(bf16)
        packed = jnp.concatenate([packed, packed], axis=1)
        left_out[i * LANES : (i + 1) * LANES, :] = packed
        image = jnp.dot(packed, gram_rows, preferred_element_type=f32)
        norm_rows = norm_rows + jnp.sum(resid * image, axis=0, keepdims=True)
        curv_rows = curv_rows + jnp.sum(weight * (image * image), axis=0, keepdims=True)
    norm = 0.5 * jnp.sum(norm_rows, axis=1, keepdims=True)
    curv = 0.5 * jnp.sum(curv_rows, axis=1, keepdims=True)
    share = jnp.where(share_lane == total, norm, share)
    share = jnp.where(share_lane == total + 1, curv, share)
    own_share = pl.ds(pl.multiple_of(me * ROWS, ROWS), ROWS)
    share_buf[own_share, :] = share

    def share_copy(step, to_other):
        other = lax.rem(me + step, count) if to_other else lax.rem(me - step + count, count)
        place = me if to_other else other
        return pltpu.make_async_remote_copy(
            src_ref=share_buf.at[own_share],
            dst_ref=share_buf.at[pl.ds(pl.multiple_of(place * ROWS, ROWS), ROWS)],
            send_sem=share_send.at[step],
            recv_sem=share_recv.at[step],
            device_id=(other // sl_count, lax.rem(other, sl_count)),
            device_id_type=MESH,
        )

    def start_share(step, carry):
        share_copy(step, True).start()
        return carry

    def wait_share(step, carry):
        share_copy(step, False).wait_recv()
        return carry

    def wait_sent(step, carry):
        spec_copy(step).wait_send()
        share_copy(step, True).wait_send()
        return carry

    lax.fori_loop(1, count, start_share, 0)
    lax.fori_loop(1, count, wait_share, 0)
    summed = share_buf[pl.ds(0, ROWS), :]
    for source in range(1, count):
        summed = summed + share_buf[pl.ds(source * ROWS, ROWS), :]
    table_out[...] = summed
    band_copy.wait_send()
    lax.fori_loop(1, count, wait_sent, 0)


def update_kernel(lane, table, left, harm, coef, out):
    norm = table[0:1, lane : lane + 1]
    curv = table[0:1, lane + 1 : lane + 2]
    step_size = norm / (curv + small_eps)
    grad = jnp.dot(left[...], harm[0], preferred_element_type=f32)
    out[0] = coef[0] - step_size * grad


def fused_shards(projections, partner, offsets, angles, coefficients):
    ang_count = lax.axis_size("ang")
    sl_count = lax.axis_size("sl")
    count = ang_count * sl_count
    per_dev, rows_dev = projections.shape[0], projections.shape[1]
    total = per_dev * ang_count
    harmonics = coefficients.shape[3]
    columns = ROWS * coefficients.shape[2]
    first, twist, last = transform_tables()
    coef = coefficients.reshape(2, columns, harmonics)
    smem = pl.BlockSpec(memory_space=pltpu.SMEM)
    vmem = pl.BlockSpec(memory_space=pltpu.VMEM)
    block = 2 * per_dev * rows_dev
    left, harm, table = pl.pallas_call(
        functools.partial(residual_kernel, ang_count, sl_count),
        out_shape=(
            jax.ShapeDtypeStruct((columns, 8 * total), bf16),
            jax.ShapeDtypeStruct((2, 8 * total, harmonics), bf16),
            jax.ShapeDtypeStruct((ROWS, LANES), f32),
        ),
        in_specs=[smem, smem, smem, vmem, vmem, vmem, vmem, pl.BlockSpec(memory_space=pl.ANY)],
        out_specs=(vmem, vmem, vmem),
        scratch_shapes=[
            pltpu.VMEM((2, columns, harmonics), f32),
            pltpu.VMEM((columns, LANES), f32),
            pltpu.VMEM((per_dev, rows_dev, EXTRA), f32),
            pltpu.VMEM((per_dev * rows_dev * HALF // LANES, LANES), f32),
            pltpu.VMEM((count * block, LANES), f32),
            pltpu.VMEM((count * block, LANES), f32),
            pltpu.VMEM((count * ROWS, LANES), f32),
            pltpu.VMEM((2, 4 * total, harmonics), bf16),
            pltpu.SemaphoreType.DMA((2, 4)),
            pltpu.SemaphoreType.DMA,
            pltpu.SemaphoreType.DMA,
            pltpu.SemaphoreType.DMA((count,)),
            pltpu.SemaphoreType.DMA((count,)),
            pltpu.SemaphoreType.DMA((count,)),
            pltpu.SemaphoreType.DMA((count,)),
        ],
        compiler_params=pltpu.CompilerParams(
            collective_id=0, has_side_effects=True, vmem_limit_bytes=40 * 2**20
        ),
        name="residual",
    )(
        partner,
        offsets,
        angles,
        projections,
        jnp.asarray(first),
        jnp.asarray(twist),
        jnp.asarray(last),
        coef,
    )
    rows_step = LANES
    updated = pl.pallas_call(
        functools.partial(update_kernel, total),
        grid=(2, columns // rows_step),
        out_shape=jax.ShapeDtypeStruct(coef.shape, f32),
        in_specs=[
            pl.BlockSpec((ROWS, LANES), lambda part, at: (0, 0)),
            pl.BlockSpec((rows_step, 8 * total), lambda part, at: (at, 0)),
            pl.BlockSpec((1, 8 * total, harmonics), lambda part, at: (part, 0, 0)),
            pl.BlockSpec((1, rows_step, harmonics), lambda part, at: (part, at, 0)),
        ],
        out_specs=pl.BlockSpec((1, rows_step, harmonics), lambda part, at: (part, at, 0)),
        compiler_params=pltpu.CompilerParams(vmem_limit_bytes=24 * 2**20),
        name="update",
    )(table, left, harm, coef)
    by_place = table[:, :total].reshape(ROWS, per_dev, ang_count)
    own = lax.dynamic_slice(
        by_place,
        (lax.axis_index("sl") * rows_dev, 0, lax.axis_index("ang")),
        (rows_dev, per_dev, 1),
    )
    return (updated.reshape(coefficients.shape), own[:, :, 0].T)


def any_shards(projections, partner, offsets, angles, coefficients):
    total = projections.shape[0] * lax.axis_size("ang")
    whole_lanes = coefficients.shape[2] == LANES and 4 * total == LANES
    run = fused_shards if whole_lanes else shards
    return run(projections, partner, offsets, angles, coefficients)


def solution(mesh):
    placed = (P("ang", "sl", None), P(), P("ang"), P(), P(None, None, ("ang", "sl"), None))
    return jax.shard_map(
        any_shards,
        mesh=mesh,
        in_specs=placed,
        out_specs=(P(None, None, ("ang", "sl"), None), P("ang", "sl")),
        check_vma=False,
    )
```

profile of v0, /device:TPU:0, one launch (start us, length us, event | category | flops | bytes accessed | tf_op | source)
XLA Modules:
  0.0 46.4 jit_solution(5374997518045620613)
XLA Ops:
  0.6 0.0 copy-start
  0.6 4.0 %copy-done = f32[2,8,128,1280]{3,2,1,0:T(8,128)S(1)} copy-done((f32[2,8,128,1280]{3,2,1,0:T(8,128)S(1)}, f32[2,8,128,1280]{3,2,1,0:T(8,128)}, u32[]{:S(2)}) %copy-start) | copy-done | bytes 10485784
  4.6 0.0 copy-start.1
  4.6 0.9 %copy-done.1 = f32[2,4,4352]{2,1,0:T(4,128)S(1)} copy-done((f32[2,4,4352]{2,1,0:T(4,128)S(1)}, f32[2,4,4352]{2,1,0:T(4,128)}, u32[]{:S(2)}) %copy-start.1) | copy-done | bytes 139288
  5.5 0.0 copy-start.2
  5.5 0.9 %copy-done.2 = f32[2,128,128]{2,1,0:T(8,128)S(1)} copy-done((f32[2,128,128]{2,1,0:T(8,128)S(1)}, f32[2,128,128]{2,1,0:T(8,128)}, u32[]{:S(2)}) %copy-start.2) | copy-done | bytes 131096
  6.4 0.0 copy-start.3
  6.4 0.8 %copy-done.3 = bf16[128,256]{1,0:T(8,128)(2,1)S(1)} copy-done((bf16[128,256]{1,0:T(8,128)(2,1)S(1)}, bf16[128,256]{1,0:T(8,128)(2,1)}, u32[]{:S(2)}) %copy-start.3) | copy-done | bytes 65560
  7.3 0.0 copy-start.4
  7.3 0.8 %copy-done.4 = bf16[128,128]{1,0:T(8,128)(2,1)S(1)} copy-done((bf16[128,128]{1,0:T(8,128)(2,1)S(1)}, bf16[128,128]{1,0:T(8,128)(2,1)}, u32[]{:S(2)}) %copy-start.4) | copy-done | bytes 32792
  8.0 0.0 copy-start.5
  8.0 0.7 %copy-done.5 = s32[32]{0:T(128)S(1)} copy-done((s32[32]{0:T(128)S(1)}, s32[32]{0:T(128)}, u32[]{:S(2)}) %copy-start.5) | copy-done | bytes 152
  8.7 0.0 copy-start.6
  8.7 0.7 %copy-done.6 = s32[2]{0:T(128)S(1)} copy-done((s32[2]{0:T(128)S(1)}, s32[2]{0:T(128)}, u32[]{:S(2)}) %copy-start.6) | copy-done | bytes 32
  9.3 0.0 copy-start.7
  9.3 0.7 %copy-done.7 = f32[32]{0:T(128)S(1)} copy-done((f32[32]{0:T(128)S(1)}, f32[32]{0:T(128)}, u32[]{:S(2)}) %copy-start.7) | copy-done | bytes 152
  10.0 26.5 %residual.1 = (bf16[1024,256]{1,0:T(8,128)(2,1)S(1)}, bf16[2,256,1280]{2,1,0:T(8,128)(2,1)S(1)}, f32[8,128]{1,0:T(8,128)S(1)}) custom-call(s32[32]{0:T(128)S(1)} %copy-done.5, s32[2]{0:T(128)S(1)} %copy-done.6, f32[32]{0:T(128)S(1)} %copy-done.7, f32[2,4,4352]{2,1,0:T(4,128)S(1)} %copy-done.1, bf16[128,128]{1,0:T(8,128)(2,1)S(1)} %copy-done.4, ...), custom_call_target="tpu_custom_call" | custom-call | tf_op jit(solution)/shard_map/residual/pallas_call | solution.py:637
  36.5 9.1 %update.1 = f32[2,1024,1280]{2,1,0:T(8,128)} custom-call(f32[8,128]{1,0:T(8,128)S(1)} %get-tuple-element.5.table, bf16[1024,256]{1,0:T(8,128)(2,1)S(1)} %get-tuple-element.6.left, bf16[2,256,1280]{2,1,0:T(8,128)(2,1)S(1)} %get-tuple-element.7.harm, f32[2,1024,1280]{2,1,0:T(8,128)S(1)} %bitcast.7), custom_call_target="tpu_custom_call" | custom-call | tf_op jit(solution)/shard_map/update/pallas_call | solution.py:678
  45.6 0.1 reshape.15
  45.7 0.1 constant_dynamic-slice_fusion
  45.8 0.7 %copy.11 = f32[4,2,1]{0,1,2:T(2,128)} copy(f32[4,2,1]{2,1,0:T(2,128)S(1)} %constant_dynamic-slice_fusion) | data formatting | bytes 64
Async XLA Ops:
  0.6 4.0 %copy-start = (f32[2,8,128,1280]{3,2,1,0:T(8,128)S(1)}, f32[2,8,128,1280]{3,2,1,0:T(8,128)}, u32[]{:S(2)}) copy-start(f32[2,8,128,1280]{3,2,1,0:T(8,128)} %param.12) | copy-start | bytes 31457284
  4.6 0.9 %copy-start.1 = (f32[2,4,4352]{2,1,0:T(4,128)S(1)}, f32[2,4,4352]{2,1,0:T(4,128)}, u32[]{:S(2)}) copy-start(f32[2,4,4352]{2,1,0:T(4,128)} %proj.1) | copy-start | bytes 417796
  5.5 0.9 %copy-start.2 = (f32[2,128,128]{2,1,0:T(8,128)S(1)}, f32[2,128,128]{2,1,0:T(8,128)}, u32[]{:S(2)}) copy-start(f32[2,128,128]{2,1,0:T(8,128)} %constant.23.clone.twist_tab) | copy-start | bytes 393220
  6.4 0.8 %copy-start.3 = (bf16[128,256]{1,0:T(8,128)(2,1)S(1)}, bf16[128,256]{1,0:T(8,128)(2,1)}, u32[]{:S(2)}) copy-start(bf16[128,256]{1,0:T(8,128)(2,1)} %constant.24.clone.last_tab) | copy-start | bytes 196612
  7.3 0.8 %copy-start.4 = (bf16[128,128]{1,0:T(8,128)(2,1)S(1)}, bf16[128,128]{1,0:T(8,128)(2,1)}, u32[]{:S(2)}) copy-start(bf16[128,128]{1,0:T(8,128)(2,1)} %constant.22.clone.first_tab) | copy-start | bytes 98308
  8.0 0.7 %copy-start.5 = (s32[32]{0:T(128)S(1)}, s32[32]{0:T(128)}, u32[]{:S(2)}) copy-start(s32[32]{0:T(128)} %partner.1) | copy-start | bytes 388
  8.7 0.7 %copy-start.6 = (s32[2]{0:T(128)S(1)}, s32[2]{0:T(128)}, u32[]{:S(2)}) copy-start(s32[2]{0:T(128)} %offsets.1) | copy-start | bytes 28
  9.3 0.7 %copy-start.7 = (f32[32]{0:T(128)S(1)}, f32[32]{0:T(128)}, u32[]{:S(2)}) copy-start(f32[32]{0:T(128)} %angles.1) | copy-start | bytes 388
where the time goes:
time: 46.7 us; the launch traced here: 46.4 us
  Pallas kernels  35.6 us (76%)
  local copies, waits for them, and re-layouts  10.2 us (22%)
  between operations  0.66 us (1%)
    pallas_call x1, Pallas kernels, fused_shards(): pl.pallas_call(functools.partial(residual_kernel, ang_count, sl_count), o...  26.5 us
    unnamed x17, local copies, waits for them, and re-layouts  10 us
    pallas_call x1, Pallas kernels, fused_shards(): pl.pallas_call(functools.partial(update_kernel, total), grid=(2, columns...  9.08 us

commit v1 on v0

--- a/solution.py
+++ b/solution.py
@@ -240,7 +240,7 @@
             np.concatenate([-np.sin(phase), np.cos(phase)], axis=1),
         ]
     )
-    return first, twist, np.concatenate(np_halves(last))
+    return first.astype(np.float32), twist, np.concatenate(np_halves(last)).astype(np.float32)
 
 
 def cos_sin(phase):
@@ -271,6 +271,18 @@
 def residual_kernel(
     ang_count,
     sl_count,
+    partner_in,
+    offsets_in,
+    angles_in,
+    proj_in,
+    first_in,
+    twist_in,
+    last_in,
+    coef,
+    left_out,
+    harm_out,
+    table_out,
+    coef_buf,
     partner,
     offsets,
     angles,
@@ -278,11 +290,7 @@
     first_tab,
     twist_tab,
     last_tab,
-    coef,
-    left_out,
-    harm_out,
-    table_out,
-    coef_buf,
+    load_sem,
     model_buf,
     band,
     folded,
@@ -315,24 +323,64 @@
             coef.at[part, rows], coef_buf.at[part, rows], coef_sem.at[part, index]
         )
 
+    loads = [
+        pltpu.make_async_copy(source, target, load_sem.at[index])
+        for index, (source, target) in enumerate(
+            (
+                (angles_in, angles),
+                (partner_in, partner),
+                (offsets_in, offsets),
+                (proj_in, proj),
+                (first_in, first_tab),
+                (twist_in, twist_tab),
+                (last_in, last_tab),
+            )
+        )
+    ]
+    for load in loads:
+        load.start()
     for index in range(4):
         for part in range(2):
             coef_copy(part, index).start()
 
+    def peer(far, near, sign):
+        there = lax.rem(ang + sign * far + ang_count, ang_count)
+        return there, lax.rem(sl + near, sl_count)
+
+    def each_peer(act):
+        for near in range(1, sl_count):
+            act(0, near)
+
+        def further(far, carry):
+            for near in range(sl_count):
+                act(far, near)
+            return carry
+
+        lax.fori_loop(1, ang_count, further, 0)
+
     barrier = pltpu.get_barrier_semaphore()
 
-    def greet(step, carry):
-        other = lax.rem(me + step, count)
+    def greet(far, near):
         pl.semaphore_signal(
-            barrier,
-            inc=1,
-            device_id=(other // sl_count, lax.rem(other, sl_count)),
-            device_id_type=MESH,
-        )
-        return carry
-
-    lax.fori_loop(1, count, greet, 0)
-
+            barrier, inc=1, device_id=peer(far, near, 1), device_id_type=MESH
+        )
+
+    each_peer(greet)
+
+    pl.semaphore_wait(barrier, count - 1)
+    across = lax.rem(ang + ang_count // 2, ang_count)
+    band_copy = pltpu.make_async_remote_copy(
+        src_ref=proj_in.at[:, :, pl.ds(HALF, EXTRA)],
+        dst_ref=band,
+        send_sem=band_send,
+        recv_sem=band_recv,
+        device_id=(across, sl),
+        device_id_type=MESH,
+    )
+    band_copy.start()
+
+    for load in loads:
+        load.wait()
     row_id = lax.broadcasted_iota(jnp.int32, (total, LANES), 0)
     angle_rows = jnp.zeros((total, LANES), f32)
     slot_rows = jnp.zeros((total, LANES), f32)
@@ -341,18 +389,6 @@
         hit = row_id == place
         angle_rows = jnp.where(hit, angles[g], angle_rows)
         slot_rows = jnp.where(hit, (partner[g] % per_dev).astype(f32), slot_rows)
-
-    pl.semaphore_wait(barrier, count - 1)
-    across = lax.rem(ang + ang_count // 2, ang_count)
-    band_copy = pltpu.make_async_remote_copy(
-        src_ref=proj.at[:, :, pl.ds(HALF, EXTRA)],
-        dst_ref=band,
-        send_sem=band_send,
-        recv_sem=band_recv,
-        device_id=(across, sl),
-        device_id_type=MESH,
-    )
-    band_copy.start()
 
     lane_id = lax.broadcasted_iota(jnp.int32, (total, LANES), 1)
     scale = 1.0 / math.sqrt(harmonics)
@@ -387,18 +423,22 @@
     gram_high, gram_low = halves(gram)
     gram_rows = jnp.concatenate([gram_high, gram_high, gram_low, gram_low], axis=0)
 
-    band_copy.wait_recv()
     flip = (
         lax.broadcasted_iota(jnp.int32, (EXTRA, EXTRA), 0)
         + lax.broadcasted_iota(jnp.int32, (EXTRA, EXTRA), 1)
         == EXTRA - 1
-    ).astype(f32)
-    mirrored = jnp.dot(
-        jnp.concatenate([band[g] for g in range(per_dev)], axis=0),
-        flip,
-        precision=highest,
-        preferred_element_type=f32,
-    )
+    )
+    flip = jnp.where(flip, 1.0, 0.0).astype(bf16)
+    band_copy.wait_recv()
+    arrived = jnp.concatenate([band[g] for g in range(per_dev)], axis=0)
+    high = arrived.astype(bf16)
+    rest = arrived - high.astype(f32)
+    middle = rest.astype(bf16)
+    low = (rest - middle.astype(f32)).astype(bf16)
+    thirds = jnp.dot(
+        jnp.concatenate([high, middle, low], axis=0), flip, preferred_element_type=f32
+    )
+    mirrored = (thirds[2 * own_rows :] + thirds[own_rows : 2 * own_rows]) + thirds[:own_rows]
     position = lax.broadcasted_iota(jnp.int32, (rows_dev, EXTRA), 1).astype(f32)
     for g in range(per_dev):
         slot = partner[ang * per_dev + g] % per_dev
@@ -421,10 +461,10 @@
         high, low = halves(folded[pl.ds(row * outer, outer), :])
         row_parts.append(jnp.concatenate([high, low, high, low], axis=0))
     first = jnp.dot(
-        first_tab[...], jnp.concatenate(row_parts, axis=1), preferred_element_type=f32
+        first_tab[...].astype(bf16), jnp.concatenate(row_parts, axis=1), preferred_element_type=f32
     )
     twist_cos, twist_sin = twist_tab[0], twist_tab[1]
-    last = last_tab[...]
+    last = last_tab[...].astype(bf16)
     freqs = K // LANES
     for row in range(own_rows):
         real = first[:64, row * LANES : (row + 1) * LANES]
@@ -445,33 +485,20 @@
 
     block = 2 * own_rows
 
-    def spec_copy(step):
-        other = lax.rem(me + step, count)
+    def spec_copy(far, near, sign):
+        there = peer(far, near, sign)
+        other = there[0] * sl_count + there[1]
+        place = me if sign > 0 else other
         return pltpu.make_async_remote_copy(
             src_ref=send_buf.at[pl.ds(pl.multiple_of(other * block, block), block)],
-            dst_ref=recv_buf.at[pl.ds(pl.multiple_of(me * block, block), block)],
-            send_sem=spec_send.at[step],
-            recv_sem=spec_recv.at[step],
-            device_id=(other // sl_count, lax.rem(other, sl_count)),
+            dst_ref=recv_buf.at[pl.ds(pl.multiple_of(place * block, block), block)],
+            send_sem=spec_send.at[far * sl_count + near],
+            recv_sem=spec_recv.at[far * sl_count + near],
+            device_id=there,
             device_id_type=MESH,
         )
 
-    def spec_arrival(step):
-        source = lax.rem(me - step + count, count)
-        return pltpu.make_async_remote_copy(
-            src_ref=send_buf.at[pl.ds(pl.multiple_of(source * block, block), block)],
-            dst_ref=recv_buf.at[pl.ds(pl.multiple_of(source * block, block), block)],
-            send_sem=spec_send.at[step],
-            recv_sem=spec_recv.at[step],
-            device_id=(source // sl_count, lax.rem(source, sl_count)),
-            device_id_type=MESH,
-        )
-
-    def start_spec(step, carry):
-        spec_copy(step).start()
-        return carry
-
-    lax.fori_loop(1, count, start_spec, 0)
+    each_peer(lambda far, near: spec_copy(far, near, 1).start())
     mine = pl.ds(pl.multiple_of(me * block, block), block)
     recv_buf[mine, :] = send_buf[mine, :]
 
@@ -507,11 +534,7 @@
             entry = entry + 2.0 * math.cos(2.0 * math.pi * q * apart / ROWS) * damping[q]
         mix.append(entry / ROWS)
 
-    def wait_spec(step, carry):
-        spec_arrival(step).wait_recv()
-        return carry
-
-    lax.fori_loop(1, count, wait_spec, 0)
+    each_peer(lambda far, near: spec_copy(far, near, -1).wait_recv())
 
     def rows_of(part, g, i):
         s, low_i = i // rows_dev, i % rows_dev
@@ -578,47 +601,64 @@
     own_share = pl.ds(pl.multiple_of(me * ROWS, ROWS), ROWS)
     share_buf[own_share, :] = share
 
-    def share_copy(step, to_other):
-        other = lax.rem(me + step, count) if to_other else lax.rem(me - step + count, count)
-        place = me if to_other else other
+    def share_copy(far, near, sign):
+        there = peer(far, near, sign)
+        place = me if sign > 0 else there[0] * sl_count + there[1]
         return pltpu.make_async_remote_copy(
             src_ref=share_buf.at[own_share],
             dst_ref=share_buf.at[pl.ds(pl.multiple_of(place * ROWS, ROWS), ROWS)],
-            send_sem=share_send.at[step],
-            recv_sem=share_recv.at[step],
-            device_id=(other // sl_count, lax.rem(other, sl_count)),
+            send_sem=share_send.at[far * sl_count + near],
+            recv_sem=share_recv.at[far * sl_count + near],
+            device_id=there,
             device_id_type=MESH,
         )
 
-    def start_share(step, carry):
-        share_copy(step, True).start()
-        return carry
-
-    def wait_share(step, carry):
-        share_copy(step, False).wait_recv()
-        return carry
-
-    def wait_sent(step, carry):
-        spec_copy(step).wait_send()
-        share_copy(step, True).wait_send()
-        return carry
-
-    lax.fori_loop(1, count, start_share, 0)
-    lax.fori_loop(1, count, wait_share, 0)
+    each_peer(lambda far, near: share_copy(far, near, 1).start())
+    band_copy.wait_send()
+    each_peer(lambda far, near: spec_copy(far, near, 1).wait_send())
+    each_peer(lambda far, near: share_copy(far, near, -1).wait_recv())
     summed = share_buf[pl.ds(0, ROWS), :]
     for source in range(1, count):
         summed = summed + share_buf[pl.ds(source * ROWS, ROWS), :]
     table_out[...] = summed
-    band_copy.wait_send()
-    lax.fori_loop(1, count, wait_sent, 0)
-
-
-def update_kernel(lane, table, left, harm, coef, out):
-    norm = table[0:1, lane : lane + 1]
-    curv = table[0:1, lane + 1 : lane + 2]
+    each_peer(lambda far, near: share_copy(far, near, 1).wait_send())
+
+
+def update_kernel(ang_count, per_dev, table, left, harm, coef, out, misfit, buf, rows_buf, sem):
+    total = ang_count * per_dev
+    columns = coef.shape[1]
+    rows_dev = rows_buf.shape[1]
+    chunk = columns // 4
+    values = table[...]
+    norm = values[0:1, total : total + 1]
+    curv = values[0:1, total + 1 : total + 2]
     step_size = norm / (curv + small_eps)
-    grad = jnp.dot(left[...], harm[0], preferred_element_type=f32)
-    out[0] = coef[0] - step_size * grad
+    copies = []
+    for index in range(4):
+        rows = slice(index * chunk, (index + 1) * chunk)
+        for part in range(2):
+            grad = jnp.dot(left[rows], harm[part], preferred_element_type=f32)
+            buf[part, rows] = coef[part, rows] - step_size * grad
+            at = pl.ds(index * chunk, chunk)
+            copy = pltpu.make_async_copy(buf.at[part, at], out.at[part, at], sem.at[part, index])
+            copy.start()
+            copies.append(copy)
+    ang = lax.axis_index("ang")
+    first_row = lax.axis_index("sl") * rows_dev
+    lane = lax.broadcasted_iota(jnp.int32, values.shape, 1)
+    row_at = lax.broadcasted_iota(jnp.int32, (ROWS, rows_dev), 0)
+    row_to = lax.broadcasted_iota(jnp.int32, (ROWS, rows_dev), 1)
+    for g in range(per_dev):
+        column = jnp.sum(
+            jnp.where(lane == g * ang_count + ang, values, 0.0), axis=1, keepdims=True
+        )
+        moved = jnp.where(row_at == row_to + first_row, column, 0.0)
+        rows_buf[g : g + 1, :] = jnp.sum(moved, axis=0, keepdims=True)
+    copy = pltpu.make_async_copy(rows_buf, misfit, sem.at[0, 4])
+    copy.start()
+    copies.append(copy)
+    for copy in copies:
+        copy.wait()
 
 
 def fused_shards(projections, partner, offsets, angles, coefficients):
@@ -631,20 +671,28 @@
     columns = ROWS * coefficients.shape[2]
     first, twist, last = transform_tables()
     coef = coefficients.reshape(2, columns, harmonics)
-    smem = pl.BlockSpec(memory_space=pltpu.SMEM)
+    hbm = pl.BlockSpec(memory_space=pltpu.HBM)
     vmem = pl.BlockSpec(memory_space=pltpu.VMEM)
     block = 2 * per_dev * rows_dev
-    left, harm, table = pl.pallas_call(
+    left, harm, table, held = pl.pallas_call(
         functools.partial(residual_kernel, ang_count, sl_count),
         out_shape=(
             jax.ShapeDtypeStruct((columns, 8 * total), bf16),
             jax.ShapeDtypeStruct((2, 8 * total, harmonics), bf16),
             jax.ShapeDtypeStruct((ROWS, LANES), f32),
+            jax.ShapeDtypeStruct(coef.shape, f32),
         ),
-        in_specs=[smem, smem, smem, vmem, vmem, vmem, vmem, pl.BlockSpec(memory_space=pl.ANY)],
-        out_specs=(vmem, vmem, vmem),
+        in_specs=[hbm] * 8,
+        out_specs=(vmem, vmem, vmem, vmem),
         scratch_shapes=[
-            pltpu.VMEM((2, columns, harmonics), f32),
+            pltpu.SMEM(partner.shape, jnp.int32),
+            pltpu.SMEM(offsets.shape, jnp.int32),
+            pltpu.SMEM(angles.shape, f32),
+            pltpu.VMEM(projections.shape, f32),
+            pltpu.VMEM(first.shape, f32),
+            pltpu.VMEM(twist.shape, f32),
+            pltpu.VMEM(last.shape, f32),
+            pltpu.SemaphoreType.DMA((7,)),
             pltpu.VMEM((columns, LANES), f32),
             pltpu.VMEM((per_dev, rows_dev, EXTRA), f32),
             pltpu.VMEM((per_dev * rows_dev * HALF // LANES, LANES), f32),
@@ -661,41 +709,41 @@
             pltpu.SemaphoreType.DMA((count,)),
         ],
         compiler_params=pltpu.CompilerParams(
-            collective_id=0, has_side_effects=True, vmem_limit_bytes=40 * 2**20
+            collective_id=0, has_side_effects=True, vmem_limit_bytes=24 * 2**20
         ),
         name="residual",
     )(
-        partner,
-        offsets,
-        angles,
-        projections,
-        jnp.asarray(first),
-        jnp.asarray(twist),
-        jnp.asarray(last),
-        coef,
-    )
-    rows_step = LANES
-    updated = pl.pallas_call(
-        functools.partial(update_kernel, total),
-        grid=(2, columns // rows_step),
-        out_shape=jax.ShapeDtypeStruct(coef.shape, f32),
-        in_specs=[
-            pl.BlockSpec((ROWS, LANES), lambda part, at: (0, 0)),
-            pl.BlockSpec((rows_step, 8 * total), lambda part, at: (at, 0)),
-            pl.BlockSpec((1, 8 * total, harmonics), lambda part, at: (part, 0, 0)),
-            pl.BlockSpec((1, rows_step, harmonics), lambda part, at: (part, at, 0)),
+        *[
+            pltpu.with_memory_space_constraint(jnp.asarray(operand), pltpu.HBM)
+            for operand in (
+                partner,
+                offsets,
+                angles,
+                projections,
+                first,
+                twist,
+                last,
+                coef,
+            )
+        ]
+    )
+    updated, misfit = pl.pallas_call(
+        functools.partial(update_kernel, ang_count, per_dev),
+        out_shape=(
+            jax.ShapeDtypeStruct(coef.shape, f32),
+            jax.ShapeDtypeStruct((per_dev, rows_dev), f32),
+        ),
+        in_specs=[vmem, vmem, vmem, vmem],
+        out_specs=(hbm, hbm),
+        scratch_shapes=[
+            pltpu.VMEM(coef.shape, f32),
+            pltpu.VMEM((per_dev, rows_dev), f32),
+            pltpu.SemaphoreType.DMA((2, 5)),
         ],
-        out_specs=pl.BlockSpec((1, rows_step, harmonics), lambda part, at: (part, at, 0)),
         compiler_params=pltpu.CompilerParams(vmem_limit_bytes=24 * 2**20),
         name="update",
-    )(table, left, harm, coef)
-    by_place = table[:, :total].reshape(ROWS, per_dev, ang_count)
-    own = lax.dynamic_slice(
-        by_place,
-        (lax.axis_index("sl") * rows_dev, 0, lax.axis_index("ang")),
-        (rows_dev, per_dev, 1),
-    )
-    return (updated.reshape(coefficients.shape), own[:, :, 0].T)
+    )(table, left, harm, held)
+    return (updated.reshape(coefficients.shape), misfit)
 
 
 def any_shards(projections, partner, offsets, angles, coefficients):

time: 46.7 us -> 30.2 us (0.65)
  local copies, waits for them, and re-layouts: 10.2 us -> 0 us
  Pallas kernels: 35.6 us -> 29.4 us
    unnamed x17 -> x0, local copies, waits for them, and re-layouts: 10 us -> none
    pallas_call x1, Pallas kernels: 9.08 us -> 4.5 us  [fused_shards(): pl.pallas_call(functools.partial(update_kernel, ang_count, per_dev), out_...]
    pallas_call x1, Pallas kernels: 26.5 us -> 24.9 us  [fused_shards(): pl.pallas_call(functools.partial(residual_kernel, ang_count, sl_count), o...]
where the time goes in v1:
time: 30.2 us; the launch traced here: 30.1 us
  Pallas kernels  29.4 us (97%)
  between operations  0.64 us (2%)
    pallas_call x1, Pallas kernels, fused_shards(): pl.pallas_call(functools.partial(residual_kernel, ang_count, sl_count), o...  24.9 us
    pallas_call x1, Pallas kernels, fused_shards(): pl.pallas_call(functools.partial(update_kernel, ang_count, per_dev), out_...  4.5 us

profile of v1, /device:TPU:0, one launch (start us, length us, event | category | flops | bytes accessed | tf_op | source)
XLA Modules:
  0.0 30.1 jit_solution(13289032945176239973)
XLA Ops:
  0.6 24.9 %residual.1 = (bf16[1024,256]{1,0:T(8,128)(2,1)S(1)}, bf16[2,256,1280]{2,1,0:T(8,128)(2,1)S(1)}, f32[8,128]{1,0:T(8,128)S(1)}, f32[2,1024,1280]{2,1,0:T(8,128)S(1)}) custom-call(s32[32]{0:T(128)} %partner_in.1, s32[2]{0:T(128)} %offsets_in.1, f32[32]{0:T(128)} %angles_in.1, f32[2,4,4352]{2,1,0:T(4,128)} %proj_in.1, f32[128,128]{1,0:T(8,128)} %constant.6.clone.first_in, ...), custom_call_target="tpu_custom_call" | custom-call | tf_op jit(solution)/shard_map/residual/pallas_call | solution.py:677
  25.6 4.5 %update.1 = (f32[2,1024,1280]{2,1,0:T(8,128)}, f32[2,4]{1,0:T(2,128)}) custom-call(f32[8,128]{1,0:T(8,128)S(1)} %get-tuple-element.8.table, bf16[1024,256]{1,0:T(8,128)(2,1)S(1)} %get-tuple-element.9.left, bf16[2,256,1280]{2,1,0:T(8,128)(2,1)S(1)} %get-tuple-element.10.harm, f32[2,1024,1280]{2,1,0:T(8,128)S(1)} %get-tuple-element.11.coef), custom_call_target="tpu_custom_call" | custom-call | tf_op jit(solution)/shard_map/update/pallas_call | solution.py:730

commit v2 on v1

--- a/solution.py
+++ b/solution.py
@@ -279,8 +279,7 @@
     twist_in,
     last_in,
     coef,
-    left_out,
-    harm_out,
+    grad_out,
     table_out,
     coef_buf,
     partner,
@@ -297,7 +296,8 @@
     send_buf,
     recv_buf,
     share_buf,
-    harm_rows,
+    left_buf,
+    harm_buf,
     coef_sem,
     band_send,
     band_recv,
@@ -392,9 +392,11 @@
 
     lane_id = lax.broadcasted_iota(jnp.int32, (total, LANES), 1)
     scale = 1.0 / math.sqrt(harmonics)
-    for tile in range(harmonics // LANES):
-        at = pl.ds(tile * LANES, LANES)
-        shift = (lane_id + (tile * LANES - harmonics // 2)).astype(f32)
+
+    def harmonic_tile(tile, carry):
+        first_lane = pl.multiple_of(tile * LANES, LANES)
+        at = pl.ds(first_lane, LANES)
+        shift = (lane_id + (first_lane - harmonics // 2)).astype(f32)
         cos_tab, sin_tab = cos_sin(angle_rows * shift)
         cos_tab = cos_tab * scale
         sin_tab = sin_tab * scale
@@ -405,8 +407,10 @@
             )
         ):
             high, low = halves(stacked)
-            harm_rows[part, :, at] = jnp.concatenate([high, low], axis=0)
-            harm_out[part, :, at] = jnp.concatenate([high, high, low, low], axis=0)
+            harm_buf[part, :, at] = jnp.concatenate([high, high, low, low], axis=0)
+        return carry
+
+    lax.fori_loop(0, harmonics // LANES, harmonic_tile, 0)
 
     flat_lanes = (HALF - EXTRA) // LANES
     outer = HALF // LANES
@@ -415,14 +419,6 @@
             folded[pl.ds(g * rows_dev * outer + tile, rows_dev, stride=outer), :] = proj[
                 g, :, pl.ds(tile * LANES, LANES)
             ]
-    gram = lax.dot_general(harm_rows[0], harm_rows[0], NT, preferred_element_type=f32)
-    gram = gram + lax.dot_general(harm_rows[1], harm_rows[1], NT, preferred_element_type=f32)
-    width = 2 * total
-    gram = gram[:width] + gram[width:]
-    gram = gram + pltpu.roll(gram, width, 1)
-    gram_high, gram_low = halves(gram)
-    gram_rows = jnp.concatenate([gram_high, gram_high, gram_low, gram_low], axis=0)
-
     flip = (
         lax.broadcasted_iota(jnp.int32, (EXTRA, EXTRA), 0)
         + lax.broadcasted_iota(jnp.int32, (EXTRA, EXTRA), 1)
@@ -466,21 +462,25 @@
     twist_cos, twist_sin = twist_tab[0], twist_tab[1]
     last = last_tab[...].astype(bf16)
     freqs = K // LANES
+    turned = []
     for row in range(own_rows):
         real = first[:64, row * LANES : (row + 1) * LANES]
         imag = first[64:, row * LANES : (row + 1) * LANES]
         real = jnp.concatenate([real, real], axis=0)
         imag = jnp.concatenate([imag, imag], axis=0)
-        turned = jnp.concatenate(
-            [real * twist_cos + imag * twist_sin, imag * twist_cos - real * twist_sin], axis=1
-        )
-        high, low = halves(turned)
-        by_high = lax.dot_general(last, high, NT, preferred_element_type=f32)
-        by_low = lax.dot_general(last[: 2 * freqs], low, NT, preferred_element_type=f32)
-        spec = by_high[: 2 * freqs] + by_high[2 * freqs :] + by_low
+        turned.append(
+            jnp.concatenate(
+                [real * twist_cos + imag * twist_sin, imag * twist_cos - real * twist_sin], axis=1
+            )
+        )
+    high, low = halves(jnp.concatenate(turned, axis=0))
+    by_high = lax.dot_general(last, high, NT, preferred_element_type=f32)
+    by_low = lax.dot_general(last[: 2 * freqs], low, NT, preferred_element_type=f32)
+    spec = by_high[: 2 * freqs] + by_high[2 * freqs :] + by_low
+    for row in range(own_rows):
         for part in range(2):
             send_buf[pl.ds(part * own_rows + row, freqs, stride=2 * own_rows), :] = spec[
-                part * freqs : (part + 1) * freqs
+                part * freqs : (part + 1) * freqs, row * LANES : (row + 1) * LANES
             ]
 
     block = 2 * own_rows
@@ -502,6 +502,22 @@
     mine = pl.ds(pl.multiple_of(me * block, block), block)
     recv_buf[mine, :] = send_buf[mine, :]
 
+    width = 2 * total
+    pair_rows = pl.ds(width, 2 * width)
+    gram = sum(
+        lax.dot_general(
+            harm_buf[part, pair_rows, :],
+            harm_buf[part, pair_rows, :],
+            NT,
+            preferred_element_type=f32,
+        )
+        for part in range(2)
+    )
+    gram = gram[:width] + gram[width:]
+    gram = gram + pltpu.roll(gram, width, 1)
+    gram_high, gram_low = halves(gram)
+    gram_rows = jnp.concatenate([gram_high, gram_high, gram_low, gram_low], axis=0)
+
     def model_chunk(index, carry):
         found = None
         for part in range(2):
@@ -509,7 +525,7 @@
             value = coef_buf[part, pl.ds(pl.multiple_of(index * chunk, chunk), chunk), :]
             high, low = halves(value)
             both = jnp.concatenate([high, low], axis=0)
-            term = lax.dot_general(both, harm_rows[part], NT, preferred_element_type=f32)
+            term = lax.dot_general(both, harm_buf[part, pair_rows, :], NT, preferred_element_type=f32)
             term = term[:chunk] + term[chunk:]
             found = term if found is None else found + term
         found = found + pltpu.roll(found, width, 1)
@@ -590,7 +606,7 @@
         high = resid.astype(bf16).astype(f32)
         packed = jnp.where(front, high, resid - high).astype(bf16)
         packed = jnp.concatenate([packed, packed], axis=1)
-        left_out[i * LANES : (i + 1) * LANES, :] = packed
+        left_buf[i * LANES : (i + 1) * LANES, :] = packed
         image = jnp.dot(packed, gram_rows, preferred_element_type=f32)
         norm_rows = norm_rows + jnp.sum(resid * image, axis=0, keepdims=True)
         curv_rows = curv_rows + jnp.sum(weight * (image * image), axis=0, keepdims=True)
@@ -614,6 +630,16 @@
         )
 
     each_peer(lambda far, near: share_copy(far, near, 1).start())
+
+    def grad_chunk(index, carry):
+        rows = pl.ds(pl.multiple_of(index * chunk, chunk), chunk)
+        for part in range(2):
+            grad_out[part, rows, :] = jnp.dot(
+                left_buf[rows, :], harm_buf[part], preferred_element_type=f32
+            )
+        return carry
+
+    lax.fori_loop(0, 4, grad_chunk, 0)
     band_copy.wait_send()
     each_peer(lambda far, near: spec_copy(far, near, 1).wait_send())
     each_peer(lambda far, near: share_copy(far, near, -1).wait_recv())
@@ -624,25 +650,30 @@
     each_peer(lambda far, near: share_copy(far, near, 1).wait_send())
 
 
-def update_kernel(ang_count, per_dev, table, left, harm, coef, out, misfit, buf, rows_buf, sem):
+def update_kernel(ang_count, per_dev, table, grad, coef, out, misfit, buf, rows_buf, sem, row_sem):
     total = ang_count * per_dev
     columns = coef.shape[1]
     rows_dev = rows_buf.shape[1]
-    chunk = columns // 4
+    pieces = 16
+    chunk = columns // pieces
     values = table[...]
     norm = values[0:1, total : total + 1]
     curv = values[0:1, total + 1 : total + 2]
     step_size = norm / (curv + small_eps)
-    copies = []
-    for index in range(4):
-        rows = slice(index * chunk, (index + 1) * chunk)
+    step_row = jnp.broadcast_to(step_size, (1, coef.shape[2]))
+
+    def piece_copy(part, index):
+        rows = pl.ds(pl.multiple_of(index * chunk, chunk), chunk)
+        return pltpu.make_async_copy(buf.at[part, rows], out.at[part, rows], sem.at[part, index])
+
+    def piece(index, carry):
+        rows = pl.ds(pl.multiple_of(index * chunk, chunk), chunk)
         for part in range(2):
-            grad = jnp.dot(left[rows], harm[part], preferred_element_type=f32)
-            buf[part, rows] = coef[part, rows] - step_size * grad
-            at = pl.ds(index * chunk, chunk)
-            copy = pltpu.make_async_copy(buf.at[part, at], out.at[part, at], sem.at[part, index])
-            copy.start()
-            copies.append(copy)
+            buf[part, rows, :] = coef[part, rows, :] - step_row * grad[part, rows, :]
+            piece_copy(part, index).start()
+        return carry
+
+    lax.fori_loop(0, pieces, piece, 0)
     ang = lax.axis_index("ang")
     first_row = lax.axis_index("sl") * rows_dev
     lane = lax.broadcasted_iota(jnp.int32, values.shape, 1)
@@ -654,11 +685,16 @@
         )
         moved = jnp.where(row_at == row_to + first_row, column, 0.0)
         rows_buf[g : g + 1, :] = jnp.sum(moved, axis=0, keepdims=True)
-    copy = pltpu.make_async_copy(rows_buf, misfit, sem.at[0, 4])
-    copy.start()
-    copies.append(copy)
-    for copy in copies:
-        copy.wait()
+    row_copy = pltpu.make_async_copy(rows_buf, misfit, row_sem)
+    row_copy.start()
+
+    def finish(index, carry):
+        for part in range(2):
+            piece_copy(part, index).wait()
+        return carry
+
+    lax.fori_loop(0, pieces, finish, 0)
+    row_copy.wait()
 
 
 def fused_shards(projections, partner, offsets, angles, coefficients):
@@ -674,16 +710,15 @@
     hbm = pl.BlockSpec(memory_space=pltpu.HBM)
     vmem = pl.BlockSpec(memory_space=pltpu.VMEM)
     block = 2 * per_dev * rows_dev
-    left, harm, table, held = pl.pallas_call(
+    grad, table, held = pl.pallas_call(
         functools.partial(residual_kernel, ang_count, sl_count),
         out_shape=(
-            jax.ShapeDtypeStruct((columns, 8 * total), bf16),
-            jax.ShapeDtypeStruct((2, 8 * total, harmonics), bf16),
+            jax.ShapeDtypeStruct(coef.shape, f32),
             jax.ShapeDtypeStruct((ROWS, LANES), f32),
             jax.ShapeDtypeStruct(coef.shape, f32),
         ),
         in_specs=[hbm] * 8,
-        out_specs=(vmem, vmem, vmem, vmem),
+        out_specs=(vmem, vmem, vmem),
         scratch_shapes=[
             pltpu.SMEM(partner.shape, jnp.int32),
             pltpu.SMEM(offsets.shape, jnp.int32),
@@ -699,7 +734,8 @@
             pltpu.VMEM((count * block, LANES), f32),
             pltpu.VMEM((count * block, LANES), f32),
             pltpu.VMEM((count * ROWS, LANES), f32),
-            pltpu.VMEM((2, 4 * total, harmonics), bf16),
+            pltpu.VMEM((columns, 8 * total), bf16),
+            pltpu.VMEM((2, 8 * total, harmonics), bf16),
             pltpu.SemaphoreType.DMA((2, 4)),
             pltpu.SemaphoreType.DMA,
             pltpu.SemaphoreType.DMA,
@@ -733,16 +769,17 @@
             jax.ShapeDtypeStruct(coef.shape, f32),
             jax.ShapeDtypeStruct((per_dev, rows_dev), f32),
         ),
-        in_specs=[vmem, vmem, vmem, vmem],
+        in_specs=[vmem, vmem, vmem],
         out_specs=(hbm, hbm),
         scratch_shapes=[
             pltpu.VMEM(coef.shape, f32),
             pltpu.VMEM((per_dev, rows_dev), f32),
-            pltpu.SemaphoreType.DMA((2, 5)),
+            pltpu.SemaphoreType.DMA((2, 16)),
+            pltpu.SemaphoreType.DMA,
         ],
         compiler_params=pltpu.CompilerParams(vmem_limit_bytes=24 * 2**20),
         name="update",
-    )(table, left, harm, held)
+    )(table, grad, held)
     return (updated.reshape(coefficients.shape), misfit)
 
 

time: 30.2 us -> 30.5 us (level)
    pallas_call x1, Pallas kernels: 24.9 us -> 25.3 us  [fused_shards(): pl.pallas_call(functools.partial(residual_kernel, ang_count, sl_count), o...]
where the time goes in v2:
time: 30.5 us; the launch traced here: 30.3 us
  Pallas kernels  29.7 us (97%)
  between operations  0.64 us (2%)
    pallas_call x1, Pallas kernels, fused_shards(): pl.pallas_call(functools.partial(residual_kernel, ang_count, sl_count), o...  25.3 us
    pallas_call x1, Pallas kernels, fused_shards(): pl.pallas_call(functools.partial(update_kernel, ang_count, per_dev), out_...  4.42 us

profile of v2, /device:TPU:0, one launch (start us, length us, event | category | flops | bytes accessed | tf_op | source)
XLA Modules:
  0.0 30.3 jit_solution(18436863770335720353)
XLA Ops:
  0.6 25.3 %residual.1 = (f32[2,1024,1280]{2,1,0:T(8,128)S(1)}, f32[8,128]{1,0:T(8,128)S(1)}, f32[2,1024,1280]{2,1,0:T(8,128)S(1)}) custom-call(s32[32]{0:T(128)} %partner_in.1, s32[2]{0:T(128)} %offsets_in.1, f32[32]{0:T(128)} %angles_in.1, f32[2,4,4352]{2,1,0:T(4,128)} %proj_in.1, f32[128,128]{1,0:T(8,128)} %constant.6.clone.first_in, ...), custom_call_target="tpu_custom_call" | custom-call | tf_op jit(solution)/shard_map/residual/pallas_call | solution.py:713
  25.9 4.4 %update.1 = (f32[2,1024,1280]{2,1,0:T(8,128)}, f32[2,4]{1,0:T(2,128)}) custom-call(f32[8,128]{1,0:T(8,128)S(1)} %get-tuple-element.7.table, f32[2,1024,1280]{2,1,0:T(8,128)S(1)} %get-tuple-element.8.grad, f32[2,1024,1280]{2,1,0:T(8,128)S(1)} %get-tuple-element.9.coef), custom_call_target="tpu_custom_call" | custom-call | tf_op jit(solution)/shard_map/update/pallas_call | solution.py:766

commit v3 on v1

--- a/solution.py
+++ b/solution.py
@@ -280,7 +280,7 @@
     last_in,
     coef,
     left_out,
-    harm_out,
+    harm_buf,
     table_out,
     coef_buf,
     partner,
@@ -297,7 +297,6 @@
     send_buf,
     recv_buf,
     share_buf,
-    harm_rows,
     coef_sem,
     band_send,
     band_recv,
@@ -348,15 +347,15 @@
         return there, lax.rem(sl + near, sl_count)
 
     def each_peer(act):
-        for near in range(1, sl_count):
-            act(0, near)
-
-        def further(far, carry):
+        def further(turn, carry):
+            far = lax.rem(turn + ang_count // 4, ang_count - 1) + 1
             for near in range(sl_count):
                 act(far, near)
             return carry
 
-        lax.fori_loop(1, ang_count, further, 0)
+        lax.fori_loop(0, ang_count - 1, further, 0)
+        for near in range(1, sl_count):
+            act(0, near)
 
     barrier = pltpu.get_barrier_semaphore()
 
@@ -392,9 +391,11 @@
 
     lane_id = lax.broadcasted_iota(jnp.int32, (total, LANES), 1)
     scale = 1.0 / math.sqrt(harmonics)
-    for tile in range(harmonics // LANES):
-        at = pl.ds(tile * LANES, LANES)
-        shift = (lane_id + (tile * LANES - harmonics // 2)).astype(f32)
+
+    def harmonic_tile(tile, carry):
+        first_lane = pl.multiple_of(tile * LANES, LANES)
+        at = pl.ds(first_lane, LANES)
+        shift = (lane_id + (first_lane - harmonics // 2)).astype(f32)
         cos_tab, sin_tab = cos_sin(angle_rows * shift)
         cos_tab = cos_tab * scale
         sin_tab = sin_tab * scale
@@ -405,8 +406,10 @@
             )
         ):
             high, low = halves(stacked)
-            harm_rows[part, :, at] = jnp.concatenate([high, low], axis=0)
-            harm_out[part, :, at] = jnp.concatenate([high, high, low, low], axis=0)
+            harm_buf[part, :, at] = jnp.concatenate([high, high, low, low], axis=0)
+        return carry
+
+    lax.fori_loop(0, harmonics // LANES, harmonic_tile, 0)
 
     flat_lanes = (HALF - EXTRA) // LANES
     outer = HALF // LANES
@@ -415,14 +418,6 @@
             folded[pl.ds(g * rows_dev * outer + tile, rows_dev, stride=outer), :] = proj[
                 g, :, pl.ds(tile * LANES, LANES)
             ]
-    gram = lax.dot_general(harm_rows[0], harm_rows[0], NT, preferred_element_type=f32)
-    gram = gram + lax.dot_general(harm_rows[1], harm_rows[1], NT, preferred_element_type=f32)
-    width = 2 * total
-    gram = gram[:width] + gram[width:]
-    gram = gram + pltpu.roll(gram, width, 1)
-    gram_high, gram_low = halves(gram)
-    gram_rows = jnp.concatenate([gram_high, gram_high, gram_low, gram_low], axis=0)
-
     flip = (
         lax.broadcasted_iota(jnp.int32, (EXTRA, EXTRA), 0)
         + lax.broadcasted_iota(jnp.int32, (EXTRA, EXTRA), 1)
@@ -466,21 +461,25 @@
     twist_cos, twist_sin = twist_tab[0], twist_tab[1]
     last = last_tab[...].astype(bf16)
     freqs = K // LANES
+    turned = []
     for row in range(own_rows):
         real = first[:64, row * LANES : (row + 1) * LANES]
         imag = first[64:, row * LANES : (row + 1) * LANES]
         real = jnp.concatenate([real, real], axis=0)
         imag = jnp.concatenate([imag, imag], axis=0)
-        turned = jnp.concatenate(
-            [real * twist_cos + imag * twist_sin, imag * twist_cos - real * twist_sin], axis=1
-        )
-        high, low = halves(turned)
-        by_high = lax.dot_general(last, high, NT, preferred_element_type=f32)
-        by_low = lax.dot_general(last[: 2 * freqs], low, NT, preferred_element_type=f32)
-        spec = by_high[: 2 * freqs] + by_high[2 * freqs :] + by_low
+        turned.append(
+            jnp.concatenate(
+                [real * twist_cos + imag * twist_sin, imag * twist_cos - real * twist_sin], axis=1
+            )
+        )
+    high, low = halves(jnp.concatenate(turned, axis=0))
+    by_high = lax.dot_general(last, high, NT, preferred_element_type=f32)
+    by_low = lax.dot_general(last[: 2 * freqs], low, NT, preferred_element_type=f32)
+    spec = by_high[: 2 * freqs] + by_high[2 * freqs :] + by_low
+    for row in range(own_rows):
         for part in range(2):
             send_buf[pl.ds(part * own_rows + row, freqs, stride=2 * own_rows), :] = spec[
-                part * freqs : (part + 1) * freqs
+                part * freqs : (part + 1) * freqs, row * LANES : (row + 1) * LANES
             ]
 
     block = 2 * own_rows
@@ -502,6 +501,22 @@
     mine = pl.ds(pl.multiple_of(me * block, block), block)
     recv_buf[mine, :] = send_buf[mine, :]
 
+    width = 2 * total
+    pair_rows = pl.ds(width, 2 * width)
+    gram = sum(
+        lax.dot_general(
+            harm_buf[part, pair_rows, :],
+            harm_buf[part, pair_rows, :],
+            NT,
+            preferred_element_type=f32,
+        )
+        for part in range(2)
+    )
+    gram = gram[:width] + gram[width:]
+    gram = gram + pltpu.roll(gram, width, 1)
+    gram_high, gram_low = halves(gram)
+    gram_rows = jnp.concatenate([gram_high, gram_high, gram_low, gram_low], axis=0)
+
     def model_chunk(index, carry):
         found = None
         for part in range(2):
@@ -509,7 +524,7 @@
             value = coef_buf[part, pl.ds(pl.multiple_of(index * chunk, chunk), chunk), :]
             high, low = halves(value)
             both = jnp.concatenate([high, low], axis=0)
-            term = lax.dot_general(both, harm_rows[part], NT, preferred_element_type=f32)
+            term = lax.dot_general(both, harm_buf[part, pair_rows, :], NT, preferred_element_type=f32)
             term = term[:chunk] + term[chunk:]
             found = term if found is None else found + term
         found = found + pltpu.roll(found, width, 1)
@@ -574,8 +589,7 @@
     share_row = lax.broadcasted_iota(jnp.int32, (ROWS, LANES), 0)
     share_lane = lax.broadcasted_iota(jnp.int32, (ROWS, LANES), 1)
     share = jnp.zeros((ROWS, LANES), f32)
-    norm_rows = jnp.zeros((1, LANES), f32)
-    curv_rows = jnp.zeros((1, LANES), f32)
+    resids = []
     front = lax.broadcasted_iota(jnp.int32, (LANES, LANES), 1) < width
     for i in range(ROWS):
         filt = mix[0] * comb[i] + mix[4] * comb[(i + 4) % ROWS]
@@ -591,9 +605,16 @@
         packed = jnp.where(front, high, resid - high).astype(bf16)
         packed = jnp.concatenate([packed, packed], axis=1)
         left_out[i * LANES : (i + 1) * LANES, :] = packed
-        image = jnp.dot(packed, gram_rows, preferred_element_type=f32)
-        norm_rows = norm_rows + jnp.sum(resid * image, axis=0, keepdims=True)
-        curv_rows = curv_rows + jnp.sum(weight * (image * image), axis=0, keepdims=True)
+        resids.append(resid)
+    images = jnp.dot(left_out[...], gram_rows, preferred_element_type=f32)
+    norm_sum = jnp.zeros((LANES, LANES), f32)
+    curv_sum = jnp.zeros((LANES, LANES), f32)
+    for i in range(ROWS):
+        image = images[i * LANES : (i + 1) * LANES]
+        norm_sum = norm_sum + resids[i] * image
+        curv_sum = curv_sum + image * image
+    norm_rows = jnp.sum(norm_sum, axis=0, keepdims=True)
+    curv_rows = jnp.sum(weight * curv_sum, axis=0, keepdims=True)
     norm = 0.5 * jnp.sum(norm_rows, axis=1, keepdims=True)
     curv = 0.5 * jnp.sum(curv_rows, axis=1, keepdims=True)
     share = jnp.where(share_lane == total, norm, share)
@@ -699,7 +720,6 @@
             pltpu.VMEM((count * block, LANES), f32),
             pltpu.VMEM((count * block, LANES), f32),
             pltpu.VMEM((count * ROWS, LANES), f32),
-            pltpu.VMEM((2, 4 * total, harmonics), bf16),
             pltpu.SemaphoreType.DMA((2, 4)),
             pltpu.SemaphoreType.DMA,
             pltpu.SemaphoreType.DMA,

time: 30.2 us -> 31.3 us (1.036)
  Pallas kernels: 29.4 us -> 30.5 us
    pallas_call x1, Pallas kernels: 24.9 us -> 26 us  [fused_shards(): pl.pallas_call(functools.partial(residual_kernel, ang_count, sl_count), o...]
where the time goes in v3:
time: 31.3 us; the launch traced here: 31.2 us
  Pallas kernels  30.5 us (97%)
  between operations  0.64 us (2%)
    pallas_call x1, Pallas kernels, fused_shards(): pl.pallas_call(functools.partial(residual_kernel, ang_count, sl_count), o...  26 us
    pallas_call x1, Pallas kernels, fused_shards(): pl.pallas_call(functools.partial(update_kernel, ang_count, per_dev), out_...  4.5 us

profile of v3, /device:TPU:0, one launch (start us, length us, event | category | flops | bytes accessed | tf_op | source)
XLA Modules:
  0.0 31.2 jit_solution(8326924019006769300)
XLA Ops:
  0.6 26.0 %residual.1 = (bf16[1024,256]{1,0:T(8,128)(2,1)S(1)}, bf16[2,256,1280]{2,1,0:T(8,128)(2,1)S(1)}, f32[8,128]{1,0:T(8,128)S(1)}, f32[2,1024,1280]{2,1,0:T(8,128)S(1)}) custom-call(s32[32]{0:T(128)} %partner_in.1, s32[2]{0:T(128)} %offsets_in.1, f32[32]{0:T(128)} %angles_in.1, f32[2,4,4352]{2,1,0:T(4,128)} %proj_in.1, f32[128,128]{1,0:T(8,128)} %constant.6.clone.first_in, ...), custom_call_target="tpu_custom_call" | custom-call | tf_op jit(solution)/shard_map/residual/pallas_call | solution.py:698
  26.7 4.5 %update.1 = (f32[2,1024,1280]{2,1,0:T(8,128)}, f32[2,4]{1,0:T(2,128)}) custom-call(f32[8,128]{1,0:T(8,128)S(1)} %get-tuple-element.8.table, bf16[1024,256]{1,0:T(8,128)(2,1)S(1)} %get-tuple-element.9.left, bf16[2,256,1280]{2,1,0:T(8,128)(2,1)S(1)} %get-tuple-element.10.harm, f32[2,1024,1280]{2,1,0:T(8,128)S(1)} %get-tuple-element.11.coef), custom_call_target="tpu_custom_call" | custom-call | tf_op jit(solution)/shard_map/update/pallas_call | solution.py:750

commit v4 on v3

--- a/solution.py
+++ b/solution.py
@@ -297,6 +297,7 @@
     send_buf,
     recv_buf,
     share_buf,
+    plane_buf,
     coef_sem,
     band_send,
     band_recv,
@@ -304,6 +305,8 @@
     spec_recv,
     share_send,
     share_recv,
+    plane_send,
+    plane_recv,
 ):
     count = ang_count * sl_count
     per_dev, rows_dev = proj.shape[0], proj.shape[1]
@@ -347,15 +350,15 @@
         return there, lax.rem(sl + near, sl_count)
 
     def each_peer(act):
-        def further(turn, carry):
-            far = lax.rem(turn + ang_count // 4, ang_count - 1) + 1
+        for near in range(1, sl_count):
+            act(0, near)
+
+        def further(far, carry):
             for near in range(sl_count):
                 act(far, near)
             return carry
 
-        lax.fori_loop(0, ang_count - 1, further, 0)
-        for near in range(1, sl_count):
-            act(0, near)
+        lax.fori_loop(1, ang_count, further, 0)
 
     barrier = pltpu.get_barrier_semaphore()
 
@@ -589,7 +592,8 @@
     share_row = lax.broadcasted_iota(jnp.int32, (ROWS, LANES), 0)
     share_lane = lax.broadcasted_iota(jnp.int32, (ROWS, LANES), 1)
     share = jnp.zeros((ROWS, LANES), f32)
-    resids = []
+    norm_rows = jnp.zeros((1, LANES), f32)
+    curv_rows = jnp.zeros((1, LANES), f32)
     front = lax.broadcasted_iota(jnp.int32, (LANES, LANES), 1) < width
     for i in range(ROWS):
         filt = mix[0] * comb[i] + mix[4] * comb[(i + 4) % ROWS]
@@ -605,44 +609,68 @@
         packed = jnp.where(front, high, resid - high).astype(bf16)
         packed = jnp.concatenate([packed, packed], axis=1)
         left_out[i * LANES : (i + 1) * LANES, :] = packed
-        resids.append(resid)
-    images = jnp.dot(left_out[...], gram_rows, preferred_element_type=f32)
-    norm_sum = jnp.zeros((LANES, LANES), f32)
-    curv_sum = jnp.zeros((LANES, LANES), f32)
-    for i in range(ROWS):
-        image = images[i * LANES : (i + 1) * LANES]
-        norm_sum = norm_sum + resids[i] * image
-        curv_sum = curv_sum + image * image
-    norm_rows = jnp.sum(norm_sum, axis=0, keepdims=True)
-    curv_rows = jnp.sum(weight * curv_sum, axis=0, keepdims=True)
+        image = jnp.dot(packed, gram_rows, preferred_element_type=f32)
+        norm_rows = norm_rows + jnp.sum(resid * image, axis=0, keepdims=True)
+        curv_rows = curv_rows + jnp.sum(weight * (image * image), axis=0, keepdims=True)
     norm = 0.5 * jnp.sum(norm_rows, axis=1, keepdims=True)
     curv = 0.5 * jnp.sum(curv_rows, axis=1, keepdims=True)
     share = jnp.where(share_lane == total, norm, share)
     share = jnp.where(share_lane == total + 1, curv, share)
-    own_share = pl.ds(pl.multiple_of(me * ROWS, ROWS), ROWS)
-    share_buf[own_share, :] = share
-
-    def share_copy(far, near, sign):
-        there = peer(far, near, sign)
-        place = me if sign > 0 else there[0] * sl_count + there[1]
+
+    planes = plane_buf.shape[0] // ROWS
+    in_plane = ang_count // planes
+    plane, inner = ang // in_plane, lax.rem(ang, in_plane)
+    members = in_plane * sl_count
+
+    def hop(buf, slot, there, send_sem, recv_sem):
+        rows = pl.ds(pl.multiple_of(slot * ROWS, ROWS), ROWS)
         return pltpu.make_async_remote_copy(
-            src_ref=share_buf.at[own_share],
-            dst_ref=share_buf.at[pl.ds(pl.multiple_of(place * ROWS, ROWS), ROWS)],
-            send_sem=share_send.at[far * sl_count + near],
-            recv_sem=share_recv.at[far * sl_count + near],
+            src_ref=buf.at[rows],
+            dst_ref=buf.at[rows],
+            send_sem=send_sem,
+            recv_sem=recv_sem,
             device_id=there,
             device_id_type=MESH,
         )
 
-    each_peer(lambda far, near: share_copy(far, near, 1).start())
+    def member_hop(step, sign):
+        far, near = step // sl_count, step % sl_count
+        there_inner = lax.rem(inner + sign * far + in_plane, in_plane)
+        there_sl = lax.rem(sl + near, sl_count)
+        slot = inner * sl_count + sl if sign > 0 else there_inner * sl_count + there_sl
+        there = (plane * in_plane + there_inner, there_sl)
+        return hop(share_buf, slot, there, share_send.at[step], share_recv.at[step])
+
+    def plane_hop(step, sign):
+        there_plane = lax.rem(plane + sign * step + planes, planes)
+        slot = plane if sign > 0 else there_plane
+        there = (there_plane * in_plane + inner, sl)
+        return hop(plane_buf, slot, there, plane_send.at[step], plane_recv.at[step])
+
+    own_rows_at = pl.multiple_of((inner * sl_count + sl) * ROWS, ROWS)
+    share_buf[pl.ds(own_rows_at, ROWS), :] = share
+    for step in range(1, members):
+        member_hop(step, 1).start()
+    for step in range(1, members):
+        member_hop(step, -1).wait_recv()
+    summed = share_buf[pl.ds(0, ROWS), :]
+    for slot in range(1, members):
+        summed = summed + share_buf[pl.ds(slot * ROWS, ROWS), :]
+    plane_buf[pl.ds(pl.multiple_of(plane * ROWS, ROWS), ROWS), :] = summed
+    for step in range(1, planes):
+        plane_hop(step, 1).start()
     band_copy.wait_send()
     each_peer(lambda far, near: spec_copy(far, near, 1).wait_send())
-    each_peer(lambda far, near: share_copy(far, near, -1).wait_recv())
-    summed = share_buf[pl.ds(0, ROWS), :]
-    for source in range(1, count):
-        summed = summed + share_buf[pl.ds(source * ROWS, ROWS), :]
+    for step in range(1, members):
+        member_hop(step, 1).wait_send()
+    for step in range(1, planes):
+        plane_hop(step, -1).wait_recv()
+    summed = plane_buf[pl.ds(0, ROWS), :]
+    for slot in range(1, planes):
+        summed = summed + plane_buf[pl.ds(slot * ROWS, ROWS), :]
     table_out[...] = summed
-    each_peer(lambda far, near: share_copy(far, near, 1).wait_send())
+    for step in range(1, planes):
+        plane_hop(step, 1).wait_send()
 
 
 def update_kernel(ang_count, per_dev, table, left, harm, coef, out, misfit, buf, rows_buf, sem):
@@ -695,6 +723,7 @@
     hbm = pl.BlockSpec(memory_space=pltpu.HBM)
     vmem = pl.BlockSpec(memory_space=pltpu.VMEM)
     block = 2 * per_dev * rows_dev
+    planes = math.gcd(ang_count, 4)
     left, harm, table, held = pl.pallas_call(
         functools.partial(residual_kernel, ang_count, sl_count),
         out_shape=(
@@ -719,14 +748,17 @@
             pltpu.VMEM((per_dev * rows_dev * HALF // LANES, LANES), f32),
             pltpu.VMEM((count * block, LANES), f32),
             pltpu.VMEM((count * block, LANES), f32),
-            pltpu.VMEM((count * ROWS, LANES), f32),
+            pltpu.VMEM((count // planes * ROWS, LANES), f32),
+            pltpu.VMEM((planes * ROWS, LANES), f32),
             pltpu.SemaphoreType.DMA((2, 4)),
             pltpu.SemaphoreType.DMA,
             pltpu.SemaphoreType.DMA,
             pltpu.SemaphoreType.DMA((count,)),
             pltpu.SemaphoreType.DMA((count,)),
-            pltpu.SemaphoreType.DMA((count,)),
-            pltpu.SemaphoreType.DMA((count,)),
+            pltpu.SemaphoreType.DMA((count // planes,)),
+            pltpu.SemaphoreType.DMA((count // planes,)),
+            pltpu.SemaphoreType.DMA((planes,)),
+            pltpu.SemaphoreType.DMA((planes,)),
         ],
         compiler_params=pltpu.CompilerParams(
             collective_id=0, has_side_effects=True, vmem_limit_bytes=24 * 2**20
@@ -769,6 +801,7 @@
 def any_shards(projections, partner, offsets, angles, coefficients):
     total = projections.shape[0] * lax.axis_size("ang")
     whole_lanes = coefficients.shape[2] == LANES and 4 * total == LANES
+    whole_lanes = whole_lanes and lax.axis_size("sl") == 2
     run = fused_shards if whole_lanes else shards
     return run(projections, partner, offsets, angles, coefficients)
 

time: 31.3 us -> 31.8 us (1.016)
  Pallas kernels: 30.5 us -> 31 us
    pallas_call x1, Pallas kernels: 26 us -> 26.5 us  [fused_shards(): pl.pallas_call(functools.partial(residual_kernel, ang_count, sl_count), o...]
where the time goes in v4:
time: 31.8 us; the launch traced here: 31.7 us
  Pallas kernels  31 us (97%)
  between operations  0.64 us (2%)
    pallas_call x1, Pallas kernels, fused_shards(): pl.pallas_call(functools.partial(residual_kernel, ang_count, sl_count), o...  26.5 us
    pallas_call x1, Pallas kernels, fused_shards(): pl.pallas_call(functools.partial(update_kernel, ang_count, per_dev), out_...  4.5 us

profile of v4, /device:TPU:0, one launch (start us, length us, event | category | flops | bytes accessed | tf_op | source)
XLA Modules:
  0.0 31.7 jit_solution(982317344377673393)
XLA Ops:
  0.6 26.5 %residual.1 = (bf16[1024,256]{1,0:T(8,128)(2,1)S(1)}, bf16[2,256,1280]{2,1,0:T(8,128)(2,1)S(1)}, f32[8,128]{1,0:T(8,128)S(1)}, f32[2,1024,1280]{2,1,0:T(8,128)S(1)}) custom-call(s32[32]{0:T(128)} %partner_in.1, s32[2]{0:T(128)} %offsets_in.1, f32[32]{0:T(128)} %angles_in.1, f32[2,4,4352]{2,1,0:T(4,128)} %proj_in.1, f32[128,128]{1,0:T(8,128)} %constant.6.clone.first_in, ...), custom_call_target="tpu_custom_call" | custom-call | tf_op jit(solution)/shard_map/residual/pallas_call | solution.py:727
  27.2 4.5 %update.1 = (f32[2,1024,1280]{2,1,0:T(8,128)}, f32[2,4]{1,0:T(2,128)}) custom-call(f32[8,128]{1,0:T(8,128)S(1)} %get-tuple-element.8.table, bf16[1024,256]{1,0:T(8,128)(2,1)S(1)} %get-tuple-element.9.left, bf16[2,256,1280]{2,1,0:T(8,128)(2,1)S(1)} %get-tuple-element.10.harm, f32[2,1024,1280]{2,1,0:T(8,128)S(1)} %get-tuple-element.11.coef), custom_call_target="tpu_custom_call" | custom-call | tf_op jit(solution)/shard_map/update/pallas_call | solution.py:782

commit v5 on v3

--- a/solution.py
+++ b/solution.py
@@ -347,15 +347,15 @@
         return there, lax.rem(sl + near, sl_count)
 
     def each_peer(act):
-        def further(turn, carry):
-            far = lax.rem(turn + ang_count // 4, ang_count - 1) + 1
+        for near in range(1, sl_count):
+            act(0, near)
+
+        def further(far, carry):
             for near in range(sl_count):
                 act(far, near)
             return carry
 
-        lax.fori_loop(0, ang_count - 1, further, 0)
-        for near in range(1, sl_count):
-            act(0, near)
+        lax.fori_loop(1, ang_count, further, 0)
 
     barrier = pltpu.get_barrier_semaphore()
 
@@ -531,7 +531,7 @@
         model_buf[pl.ds(pl.multiple_of(index * chunk, chunk), chunk), :] = found
         return carry
 
-    lax.fori_loop(0, 4, model_chunk, 0)
+    lax.fori_loop(0, 4, model_chunk, 0, unroll=True)
 
     base = (me * LANES).astype(f32)
     lane_freq = lax.broadcasted_iota(jnp.int32, (8, LANES), 1).astype(f32) + base
@@ -589,7 +589,8 @@
     share_row = lax.broadcasted_iota(jnp.int32, (ROWS, LANES), 0)
     share_lane = lax.broadcasted_iota(jnp.int32, (ROWS, LANES), 1)
     share = jnp.zeros((ROWS, LANES), f32)
-    resids = []
+    norm_rows = jnp.zeros((1, LANES), f32)
+    curv_rows = jnp.zeros((1, LANES), f32)
     front = lax.broadcasted_iota(jnp.int32, (LANES, LANES), 1) < width
     for i in range(ROWS):
         filt = mix[0] * comb[i] + mix[4] * comb[(i + 4) % ROWS]
@@ -605,16 +606,9 @@
         packed = jnp.where(front, high, resid - high).astype(bf16)
         packed = jnp.concatenate([packed, packed], axis=1)
         left_out[i * LANES : (i + 1) * LANES, :] = packed
-        resids.append(resid)
-    images = jnp.dot(left_out[...], gram_rows, preferred_element_type=f32)
-    norm_sum = jnp.zeros((LANES, LANES), f32)
-    curv_sum = jnp.zeros((LANES, LANES), f32)
-    for i in range(ROWS):
-        image = images[i * LANES : (i + 1) * LANES]
-        norm_sum = norm_sum + resids[i] * image
-        curv_sum = curv_sum + image * image
-    norm_rows = jnp.sum(norm_sum, axis=0, keepdims=True)
-    curv_rows = jnp.sum(weight * curv_sum, axis=0, keepdims=True)
+        image = jnp.dot(packed, gram_rows, preferred_element_type=f32)
+        norm_rows = norm_rows + jnp.sum(resid * image, axis=0, keepdims=True)
+        curv_rows = curv_rows + jnp.sum(weight * (image * image), axis=0, keepdims=True)
     norm = 0.5 * jnp.sum(norm_rows, axis=1, keepdims=True)
     curv = 0.5 * jnp.sum(curv_rows, axis=1, keepdims=True)
     share = jnp.where(share_lane == total, norm, share)
@@ -769,6 +763,7 @@
 def any_shards(projections, partner, offsets, angles, coefficients):
     total = projections.shape[0] * lax.axis_size("ang")
     whole_lanes = coefficients.shape[2] == LANES and 4 * total == LANES
+    whole_lanes = whole_lanes and lax.axis_size("sl") == 2
     run = fused_shards if whole_lanes else shards
     return run(projections, partner, offsets, angles, coefficients)
 

time: 31.3 us -> 30.3 us (0.968)
  Pallas kernels: 30.5 us -> 29.5 us
    pallas_call x1, Pallas kernels: 26 us -> 25 us  [fused_shards(): pl.pallas_call(functools.partial(residual_kernel, ang_count, sl_count), o...]
where the time goes in v5:
time: 30.3 us; the launch traced here: 30.1 us
  Pallas kernels  29.5 us (97%)
  between operations  0.64 us (2%)
    pallas_call x1, Pallas kernels, fused_shards(): pl.pallas_call(functools.partial(residual_kernel, ang_count, sl_count), o...  25 us
    pallas_call x1, Pallas kernels, fused_shards(): pl.pallas_call(functools.partial(update_kernel, ang_count, per_dev), out_...  4.5 us

profile of v5, /device:TPU:0, one launch (start us, length us, event | category | flops | bytes accessed | tf_op | source)
XLA Modules:
  0.0 30.1 jit_solution(3239541732077396939)
XLA Ops:
  0.6 25.0 %residual.1 = (bf16[1024,256]{1,0:T(8,128)(2,1)S(1)}, bf16[2,256,1280]{2,1,0:T(8,128)(2,1)S(1)}, f32[8,128]{1,0:T(8,128)S(1)}, f32[2,1024,1280]{2,1,0:T(8,128)S(1)}) custom-call(s32[32]{0:T(128)} %partner_in.1, s32[2]{0:T(128)} %offsets_in.1, f32[32]{0:T(128)} %angles_in.1, f32[2,4,4352]{2,1,0:T(4,128)} %proj_in.1, f32[128,128]{1,0:T(8,128)} %constant.6.clone.first_in, ...), custom_call_target="tpu_custom_call" | custom-call | tf_op jit(solution)/shard_map/residual/pallas_call | solution.py:692
  25.6 4.5 %update.1 = (f32[2,1024,1280]{2,1,0:T(8,128)}, f32[2,4]{1,0:T(2,128)}) custom-call(f32[8,128]{1,0:T(8,128)S(1)} %get-tuple-element.8.table, bf16[1024,256]{1,0:T(8,128)(2,1)S(1)} %get-tuple-element.9.left, bf16[2,256,1280]{2,1,0:T(8,128)(2,1)S(1)} %get-tuple-element.10.harm, f32[2,1024,1280]{2,1,0:T(8,128)S(1)} %get-tuple-element.11.coef), custom_call_target="tpu_custom_call" | custom-call | tf_op jit(solution)/shard_map/update/pallas_call | solution.py:744

commit v6 on v1

--- a/solution.py
+++ b/solution.py
@@ -466,6 +466,23 @@
     twist_cos, twist_sin = twist_tab[0], twist_tab[1]
     last = last_tab[...].astype(bf16)
     freqs = K // LANES
+    block = 2 * rows_dev
+
+    def spec_copy(far, near, sign, g):
+        there = peer(far, near, sign)
+        other = there[0] * sl_count + there[1]
+        place = me if sign > 0 else other
+        index = (far * sl_count + near) * per_dev + g
+        return pltpu.make_async_remote_copy(
+            src_ref=send_buf.at[g, pl.ds(pl.multiple_of(other * block, block), block)],
+            dst_ref=recv_buf.at[g, pl.ds(pl.multiple_of(place * block, block), block)],
+            send_sem=spec_send.at[index],
+            recv_sem=spec_recv.at[index],
+            device_id=there,
+            device_id_type=MESH,
+        )
+
+    mine = pl.ds(pl.multiple_of(me * block, block), block)
     for row in range(own_rows):
         real = first[:64, row * LANES : (row + 1) * LANES]
         imag = first[64:, row * LANES : (row + 1) * LANES]
@@ -479,28 +496,15 @@
         by_low = lax.dot_general(last[: 2 * freqs], low, NT, preferred_element_type=f32)
         spec = by_high[: 2 * freqs] + by_high[2 * freqs :] + by_low
         for part in range(2):
-            send_buf[pl.ds(part * own_rows + row, freqs, stride=2 * own_rows), :] = spec[
+            g, low_i = row // rows_dev, row % rows_dev
+            send_buf[g, pl.ds(part * rows_dev + low_i, freqs, stride=block), :] = spec[
                 part * freqs : (part + 1) * freqs
             ]
-
-    block = 2 * own_rows
-
-    def spec_copy(far, near, sign):
-        there = peer(far, near, sign)
-        other = there[0] * sl_count + there[1]
-        place = me if sign > 0 else other
-        return pltpu.make_async_remote_copy(
-            src_ref=send_buf.at[pl.ds(pl.multiple_of(other * block, block), block)],
-            dst_ref=recv_buf.at[pl.ds(pl.multiple_of(place * block, block), block)],
-            send_sem=spec_send.at[far * sl_count + near],
-            recv_sem=spec_recv.at[far * sl_count + near],
-            device_id=there,
-            device_id_type=MESH,
-        )
-
-    each_peer(lambda far, near: spec_copy(far, near, 1).start())
-    mine = pl.ds(pl.multiple_of(me * block, block), block)
-    recv_buf[mine, :] = send_buf[mine, :]
+        if row % rows_dev == rows_dev - 1:
+            g = row // rows_dev
+            each_peer(lambda far, near: spec_copy(far, near, 1, g).start())
+            recv_buf[g, mine, :] = send_buf[g, mine, :]
+
 
     def model_chunk(index, carry):
         found = None
@@ -534,12 +538,13 @@
             entry = entry + 2.0 * math.cos(2.0 * math.pi * q * apart / ROWS) * damping[q]
         mix.append(entry / ROWS)
 
-    each_peer(lambda far, near: spec_copy(far, near, -1).wait_recv())
+    for g in range(per_dev):
+        each_peer(lambda far, near: spec_copy(far, near, -1, g).wait_recv())
 
     def rows_of(part, g, i):
         s, low_i = i // rows_dev, i % rows_dev
-        start = s * block + part * own_rows + g * rows_dev + low_i
-        return recv_buf[pl.ds(start, ang_count, stride=sl_count * block), :]
+        start = s * block + part * rows_dev + low_i
+        return recv_buf[g, pl.ds(start, ang_count, stride=sl_count * block), :]
 
     def swapped(value):
         return jnp.concatenate([value[ang_count // 2 :], value[: ang_count // 2]], axis=0)
@@ -615,7 +620,8 @@
 
     each_peer(lambda far, near: share_copy(far, near, 1).start())
     band_copy.wait_send()
-    each_peer(lambda far, near: spec_copy(far, near, 1).wait_send())
+    for g in range(per_dev):
+        each_peer(lambda far, near: spec_copy(far, near, 1, g).wait_send())
     each_peer(lambda far, near: share_copy(far, near, -1).wait_recv())
     summed = share_buf[pl.ds(0, ROWS), :]
     for source in range(1, count):
@@ -673,7 +679,7 @@
     coef = coefficients.reshape(2, columns, harmonics)
     hbm = pl.BlockSpec(memory_space=pltpu.HBM)
     vmem = pl.BlockSpec(memory_space=pltpu.VMEM)
-    block = 2 * per_dev * rows_dev
+    block = 2 * rows_dev
     left, harm, table, held = pl.pallas_call(
         functools.partial(residual_kernel, ang_count, sl_count),
         out_shape=(
@@ -696,15 +702,15 @@
             pltpu.VMEM((columns, LANES), f32),
             pltpu.VMEM((per_dev, rows_dev, EXTRA), f32),
             pltpu.VMEM((per_dev * rows_dev * HALF // LANES, LANES), f32),
-            pltpu.VMEM((count * block, LANES), f32),
-            pltpu.VMEM((count * block, LANES), f32),
+            pltpu.VMEM((per_dev, count * block, LANES), f32),
+            pltpu.VMEM((per_dev, count * block, LANES), f32),
             pltpu.VMEM((count * ROWS, LANES), f32),
             pltpu.VMEM((2, 4 * total, harmonics), bf16),
             pltpu.SemaphoreType.DMA((2, 4)),
             pltpu.SemaphoreType.DMA,
             pltpu.SemaphoreType.DMA,
-            pltpu.SemaphoreType.DMA((count,)),
-            pltpu.SemaphoreType.DMA((count,)),
+            pltpu.SemaphoreType.DMA((count * per_dev,)),
+            pltpu.SemaphoreType.DMA((count * per_dev,)),
             pltpu.SemaphoreType.DMA((count,)),
             pltpu.SemaphoreType.DMA((count,)),
         ],

time: 30.2 us -> 31 us (1.026)
  Pallas kernels: 29.4 us -> 30.2 us
    pallas_call x1, Pallas kernels: 24.9 us -> 25.7 us  [fused_shards(): pl.pallas_call(functools.partial(residual_kernel, ang_count, sl_count), o...]
where the time goes in v6:
time: 31 us; the launch traced here: 30.8 us
  Pallas kernels  30.2 us (97%)
  between operations  0.64 us (2%)
    pallas_call x1, Pallas kernels, fused_shards(): pl.pallas_call(functools.partial(residual_kernel, ang_count, sl_count), o...  25.7 us
    pallas_call x1, Pallas kernels, fused_shards(): pl.pallas_call(functools.partial(update_kernel, ang_count, per_dev), out_...  4.5 us

profile of v6, /device:TPU:0, one launch (start us, length us, event | category | flops | bytes accessed | tf_op | source)
XLA Modules:
  0.0 30.8 jit_solution(6182806397548797090)
XLA Ops:
  0.6 25.7 %residual.1 = (bf16[1024,256]{1,0:T(8,128)(2,1)S(1)}, bf16[2,256,1280]{2,1,0:T(8,128)(2,1)S(1)}, f32[8,128]{1,0:T(8,128)S(1)}, f32[2,1024,1280]{2,1,0:T(8,128)S(1)}) custom-call(s32[32]{0:T(128)} %partner_in.1, s32[2]{0:T(128)} %offsets_in.1, f32[32]{0:T(128)} %angles_in.1, f32[2,4,4352]{2,1,0:T(4,128)} %proj_in.1, f32[128,128]{1,0:T(8,128)} %constant.6.clone.first_in, ...), custom_call_target="tpu_custom_call" | custom-call | tf_op jit(solution)/shard_map/residual/pallas_call | solution.py:683
  26.3 4.5 %update.1 = (f32[2,1024,1280]{2,1,0:T(8,128)}, f32[2,4]{1,0:T(2,128)}) custom-call(f32[8,128]{1,0:T(8,128)S(1)} %get-tuple-element.8.table, bf16[1024,256]{1,0:T(8,128)(2,1)S(1)} %get-tuple-element.9.left, bf16[2,256,1280]{2,1,0:T(8,128)(2,1)S(1)} %get-tuple-element.10.harm, f32[2,1024,1280]{2,1,0:T(8,128)S(1)} %get-tuple-element.11.coef), custom_call_target="tpu_custom_call" | custom-call | tf_op jit(solution)/shard_map/update/pallas_call | solution.py:736

commit v7 on v1

--- a/solution.py
+++ b/solution.py
@@ -423,6 +423,21 @@
     gram_high, gram_low = halves(gram)
     gram_rows = jnp.concatenate([gram_high, gram_high, gram_low, gram_low], axis=0)
 
+    def model_chunk(index, carry):
+        found = None
+        for part in range(2):
+            coef_copy(part, index).wait()
+            value = coef_buf[part, pl.ds(pl.multiple_of(index * chunk, chunk), chunk), :]
+            high, low = halves(value)
+            both = jnp.concatenate([high, low], axis=0)
+            term = lax.dot_general(both, harm_rows[part], NT, preferred_element_type=f32)
+            term = term[:chunk] + term[chunk:]
+            found = term if found is None else found + term
+        found = found + pltpu.roll(found, width, 1)
+        model_buf[pl.ds(pl.multiple_of(index * chunk, chunk), chunk), :] = found
+        return carry
+
+    lax.fori_loop(0, 1, model_chunk, 0)
     flip = (
         lax.broadcasted_iota(jnp.int32, (EXTRA, EXTRA), 0)
         + lax.broadcasted_iota(jnp.int32, (EXTRA, EXTRA), 1)
@@ -502,21 +517,7 @@
     mine = pl.ds(pl.multiple_of(me * block, block), block)
     recv_buf[mine, :] = send_buf[mine, :]
 
-    def model_chunk(index, carry):
-        found = None
-        for part in range(2):
-            coef_copy(part, index).wait()
-            value = coef_buf[part, pl.ds(pl.multiple_of(index * chunk, chunk), chunk), :]
-            high, low = halves(value)
-            both = jnp.concatenate([high, low], axis=0)
-            term = lax.dot_general(both, harm_rows[part], NT, preferred_element_type=f32)
-            term = term[:chunk] + term[chunk:]
-            found = term if found is None else found + term
-        found = found + pltpu.roll(found, width, 1)
-        model_buf[pl.ds(pl.multiple_of(index * chunk, chunk), chunk), :] = found
-        return carry
-
-    lax.fori_loop(0, 4, model_chunk, 0)
+    lax.fori_loop(1, 4, model_chunk, 0)
 
     base = (me * LANES).astype(f32)
     lane_freq = lax.broadcasted_iota(jnp.int32, (8, LANES), 1).astype(f32) + base

time: 30.2 us -> 31 us (1.026)
  Pallas kernels: 29.4 us -> 30.2 us
    pallas_call x1, Pallas kernels: 24.9 us -> 25.7 us  [fused_shards(): pl.pallas_call(functools.partial(residual_kernel, ang_count, sl_count), o...]
where the time goes in v7:
time: 31 us; the launch traced here: 30.9 us
  Pallas kernels  30.2 us (97%)
  between operations  0.64 us (2%)
    pallas_call x1, Pallas kernels, fused_shards(): pl.pallas_call(functools.partial(residual_kernel, ang_count, sl_count), o...  25.7 us
    pallas_call x1, Pallas kernels, fused_shards(): pl.pallas_call(functools.partial(update_kernel, ang_count, per_dev), out_...  4.5 us

profile of v7, /device:TPU:0, one launch (start us, length us, event | category | flops | bytes accessed | tf_op | source)
XLA Modules:
  0.0 30.9 jit_solution(5176370637688470946)
XLA Ops:
  0.6 25.7 %residual.1 = (bf16[1024,256]{1,0:T(8,128)(2,1)S(1)}, bf16[2,256,1280]{2,1,0:T(8,128)(2,1)S(1)}, f32[8,128]{1,0:T(8,128)S(1)}, f32[2,1024,1280]{2,1,0:T(8,128)S(1)}) custom-call(s32[32]{0:T(128)} %partner_in.1, s32[2]{0:T(128)} %offsets_in.1, f32[32]{0:T(128)} %angles_in.1, f32[2,4,4352]{2,1,0:T(4,128)} %proj_in.1, f32[128,128]{1,0:T(8,128)} %constant.6.clone.first_in, ...), custom_call_target="tpu_custom_call" | custom-call | tf_op jit(solution)/shard_map/residual/pallas_call | solution.py:678
  26.4 4.5 %update.1 = (f32[2,1024,1280]{2,1,0:T(8,128)}, f32[2,4]{1,0:T(2,128)}) custom-call(f32[8,128]{1,0:T(8,128)S(1)} %get-tuple-element.8.table, bf16[1024,256]{1,0:T(8,128)(2,1)S(1)} %get-tuple-element.9.left, bf16[2,256,1280]{2,1,0:T(8,128)(2,1)S(1)} %get-tuple-element.10.harm, f32[2,1024,1280]{2,1,0:T(8,128)S(1)} %get-tuple-element.11.coef), custom_call_target="tpu_custom_call" | custom-call | tf_op jit(solution)/shard_map/update/pallas_call | solution.py:731
